TPU v7x, 256 devices: a whole 4x4x8 slice. The times are simulated.
256 devices in a mesh: blk: 8 (over z), tp: 4 (over x_hi, core), rep: 8 (over x_lo, y).
Axes of the slice: x: 4 (x_hi: 2, x_lo: 2; x = x_hi * 2 + x_lo), y: 4, z: 8, core: 2. Of those that a mesh axis runs over, the one named last changes fastest.
Arguments:
- context: bfloat16 [24576, 2560], P(('blk', 'rep'), 'tp'), may hold values from -6 to 6
- out_weight: bfloat16 [5120, 2560], P('blk', 'tp'), may hold values from -0.125 to 0.125
- grad_out: bfloat16 [24576, 5120], P(('blk', 'rep'), 'tp'), may hold values from -16 to 16
Outputs:
- projected: bfloat16 [24576, 5120], P(('blk', 'rep'), 'tp')
- grad_context: bfloat16 [24576, 2560], P(('blk', 'rep'), 'tp')
- grad_weight: float32 [5120, 2560], P(('blk', 'rep'), 'tp')
All inputs are finite; a program needn't handle non-finite values.
Results may differ from a plain program's by a relative error of at most 0.015.
Values may be sent and summed in bfloat16 or wider, within the bound.
No kernel may reach another device: no remote copies, remote signals or barrier semaphores. Data moves between devices by JAX's collectives and lax.ppermute only.
A program may use at most 128 MiB of HBM per device.

v0:
```python
import jax
import jax.numpy as jnp
from jax import lax
from jax.sharding import PartitionSpec as P


def body(context, out_weight, grad_out):
    full_grad = lax.all_gather(grad_out, "tp", axis=1, tiled=True)
    contract = (((1,), (1,)), ((), ()))
    whole = lax.all_gather(out_weight, "blk", axis=0, tiled=True)
    partial_value = lax.dot_general(context, whole, contract, preferred_element_type=jnp.float32)
    grad_ctx = jnp.dot(full_grad, whole, preferred_element_type=jnp.float32)
    projected = lax.psum_scatter(
        partial_value.astype(jnp.bfloat16), "tp", scatter_dimension=1, tiled=True
    )
    grad_context = grad_ctx.astype(jnp.bfloat16)
    tokens_first = (((0,), (0,)), ((), ()))
    grad_weight = lax.psum_scatter(
        lax.dot_general(full_grad, context, tokens_first, preferred_element_type=jnp.float32),
        ("blk", "rep"),
        scatter_dimension=0,
        tiled=True,
    )
    return (projected, grad_context, grad_weight)


def solution(mesh):
    return jax.shard_map(
        body,
        mesh=mesh,
        in_specs=(P(("blk", "rep"), "tp"), P("blk", "tp"), P(("blk", "rep"), "tp")),
        out_specs=(P(("blk", "rep"), "tp"), P(("blk", "rep"), "tp"), P(("blk", "rep"), "tp")),
        check_vma=False,
    )
```

profile of v0, /device:TPU:6, one launch (start us, length us, event | category | flops | bytes accessed | tf_op | source)
XLA Modules:
  0.0 534.8 jit_solution(13749380677013191415)
XLA Ops:
  7.2 0.0 copy-start
  7.2 0.0 all-gather.3.cloned.1.call-start
  7.2 0.7 all-gather.3.cloned.1.call-update
  7.9 0.0 all-gather.5.cloned.1.call-start
  8.0 0.7 all-gather.5.cloned.1.call-update
  8.7 0.0 reduce-scatter.3.cloned.1.call-start
  8.7 81.0 %all-gather.3.cloned.1.call-done = bf16[5120,640]{1,0:T(8,128)(2,1)} async-done(((bf16[640,640]{1,0:T(8,128)(2,1)}), bf16[5120,640]{1,0:T(8,128)(2,1)}) %all-gather.3.cloned.1.call-update) | async-done | bytes 6553616 | tf_op jit(solution)/shard_map/all_gather | solution.py:10
  89.7 0.0 copy-done
  89.7 8.9 %convolution_convert_fusion = bf16[384,5120]{1,0:T(8,128)(2,1)} fusion(bf16[384,640]{1,0:T(8,128)(2,1)S(1)} %copy-done, bf16[5120,640]{1,0:T(8,128)(2,1)} %all-gather.3.cloned.1.call-done), kind=kOutput, calls=%fused_computation | convolution fusion | flops 2518548480 | bytes 10977280 | tf_op jit(solution)/shard_map/dot_general | solution.py:11
  98.6 0.0 reduce-scatter.3.cloned.1.call-update
  98.6 0.0 reduce-scatter.5.cloned.1.call-start
  98.7 29.5 %all-gather.5.cloned.1.call-done = bf16[384,5120]{1,0:T(8,128)(2,1)} async-done(((bf16[384,1280]{1,0:T(8,128)(2,1)}), bf16[384,5120]{1,0:T(8,128)(2,1)}) %all-gather.5.cloned.1.call-update) | async-done | bytes 3932176 | tf_op jit(solution)/shard_map/all_gather | solution.py:8
  128.2 10.8 %fusion = f32[5120,640]{1,0:T(8,128)} fusion(bf16[384,5120]{1,0:T(8,128)(2,1)} %all-gather.5.cloned.1.call-done, bf16[384,640]{1,0:T(8,128)(2,1)S(1)} %copy-done), kind=kOutput, calls=%fused_computation.2 | convolution fusion | flops 2516582400 | bytes 17530880 | tf_op jit(solution)/shard_map/dot_general | solution.py:19
  138.9 0.0 reduce-scatter.5.cloned.1.call-update
  139.0 8.0 %convolution_convert_fusion.1 = bf16[384,640]{1,0:T(8,128)(2,1)} fusion(bf16[384,5120]{1,0:T(8,128)(2,1)} %all-gather.5.cloned.1.call-done, bf16[5120,640]{1,0:T(8,128)(2,1)} %all-gather.3.cloned.1.call-done), kind=kOutput, calls=%fused_computation.1 | convolution fusion | flops 2516828160 | bytes 10977280 | tf_op jit(solution)/shard_map/dot_general | solution.py:12
  147.0 39.0 %reduce-scatter.3.cloned.1.call-done = bf16[384,1280]{1,0:T(8,128)(2,1)} async-done(((bf16[384,5120]{1,0:T(8,128)(2,1)}), bf16[384,1280]{1,0:T(8,128)(2,1)}) %reduce-scatter.3.cloned.1.call-update) | async-done | bytes 983056 | tf_op jit(solution)/shard_map/reduce_scatter | solution.py:13
  186.0 342.3 %reduce-scatter.5.cloned.1.call-done = f32[80,640]{1,0:T(8,128)} async-done(((f32[5120,640]{1,0:T(8,128)}), f32[80,640]{1,0:T(8,128)}) %reduce-scatter.5.cloned.1.call-update) | async-done | bytes 204816 | tf_op jit(solution)/shard_map/reduce_scatter | solution.py:18
Async XLA Ops:
  7.2 82.5 %copy-start = (bf16[384,640]{1,0:T(8,128)(2,1)S(1)}, bf16[384,640]{1,0:T(8,128)(2,1)}, u32[]{:S(2)}) copy-start(bf16[384,640]{1,0:T(8,128)(2,1)} %param.3) | copy-start | bytes 1474564
  7.2 82.5 %all-gather.3.cloned.1.call-start = ((), (), s32[]{:S(2)}) async-start(), calls=%async_computation.2 | async-start | bytes 7372800 | tf_op jit(solution)/shard_map/all_gather | solution.py:10
  7.9 120.3 %all-gather.5.cloned.1.call-start = ((), (), s32[]{:S(2)}) async-start(), calls=%async_computation.4 | async-start | bytes 4915200 | tf_op jit(solution)/shard_map/all_gather | solution.py:8
  8.7 177.3 %reduce-scatter.3.cloned.1.call-start = ((), (), s32[]{:S(2)}) async-start(), calls=%async_computation.3 | async-start | bytes 4915200 | tf_op jit(solution)/shard_map/reduce_scatter | solution.py:13
  98.6 429.6 %reduce-scatter.5.cloned.1.call-start = ((), (), s32[]{:S(2)}) async-start(), calls=%async_computation.5 | async-start | bytes 13312000 | tf_op jit(solution)/shard_map/reduce_scatter | solution.py:18
Sparse Core Ops, SparseCore 0:
  9.8 79.8 all-gather.2
  91.5 36.6 all-gather.4
  131.5 54.3 reduce-scatter.2
  189.1 339.0 reduce-scatter.4
where the time goes:
time: 543 us; the launch traced here: 535 us
  waiting for transfers between devices  493 us (91%)
  matrix products  27.7 us (5%)
  between operations  13.8 us (3%)
    reduce_scatter x1, waiting for transfers between devices, body(): lax.psum_scatter(lax.dot_general(full_grad, context, tokens_first, prefer...  342 us
    all_gather x1, waiting for transfers between devices, body(): whole = lax.all_gather(out_weight, 'blk', axis=0, tiled=True)  81 us
    reduce_scatter x1, waiting for transfers between devices, body(): lax.psum_scatter(partial_value.astype(jnp.bfloat16), 'tp', scatter_dimens...  39 us
    all_gather x1, waiting for transfers between devices, body(): full_grad = lax.all_gather(grad_out, 'tp', axis=1, tiled=True)  29.5 us
  transfers between devices with their start and end apart: 4, of which 4 were waited for; matrix products, arithmetic and copies ran while one was open for 5% of the time, Pallas kernels for 0%

commit v1 on v0

v1 whole, which is shorter than its diff:
```python
import jax
import jax.numpy as jnp
from jax import lax
from jax.sharding import PartitionSpec as P

BF, F32 = jnp.bfloat16, jnp.float32
ALL = ("blk", "tp", "rep")


def number(z, a, k, l, y):
    return (z * 4 + a * 2 + k) * 8 + l * 4 + y


def places():
    for z in range(8):
        for a in range(2):
            for k in range(2):
                for l in range(2):
                    for y in range(4):
                        yield z, a, k, l, y


def move(value, target):
    return lax.ppermute(value, ALL, [(number(*p), number(*target(*p))) for p in places()])


def core_swap(v):
    return move(v, lambda z, a, k, l, y: (z, a, 1 - k, l, y))


def x_swap(v):
    return move(v, lambda z, a, k, l, y: (z, a, k, 1 - l, y))


def dot(a, b, ca, cb):
    return lax.dot_general(a, b, (((ca,), (cb,)), ((), ())), preferred_element_type=F32)


def body(context, out_weight, grad_out):
    z = lax.axis_index("blk")
    t = lax.axis_index("tp")
    r = lax.axis_index("rep")
    a, k, h, y = t // 2, t % 2, r // 4, r % 4

    half = lax.dynamic_slice_in_dim(out_weight, h * 320, 320, 0)
    w_piece = move(half, lambda z, a, k, l, y: (2 * (z % 4) + l, z // 4, k, a, y))
    weight = lax.all_gather(w_piece, "blk", axis=0, tiled=True)

    c_a = move(context, lambda z, a, k, l, y: (z, l, k, a, y))
    c_b = move(context, lambda z, a, k, l, y: (z, 1 - l, k, a, y))
    same = a == h
    ctx = jnp.concatenate([jnp.where(same, c_a, c_b), jnp.where(same, c_b, c_a)], axis=0)

    def both(mine):
        other = core_swap(mine)
        first = k == 0
        return jnp.concatenate([jnp.where(first, mine, other), jnp.where(first, other, mine)], axis=1)

    gout_far = x_swap(grad_out)
    gout = jnp.concatenate([both(grad_out), both(gout_far)], axis=0)

    gw = dot(gout, ctx, 0, 0).astype(BF).reshape(8, 4, 80, 640)
    total = lax.dynamic_index_in_dim(gw, y, 1, keepdims=False).astype(F32)
    for d in (1, 3, 2):
        piece = lax.dynamic_index_in_dim(gw, (y + d) % 4, 1, keepdims=False)
        total += move(piece, lambda z, a, k, l, y: (z, a, k, l, (y + d) % 4)).astype(F32)
    gy = total.astype(BF)
    grad_weight = jnp.zeros((80, 640), F32)
    for d in range(8):
        piece = lax.dynamic_index_in_dim(gy, (z + d) % 8, 0, keepdims=False)

        def owner(z, a, k, l, y):
            code = (z + d) % 8
            return 4 * a + code // 2, l, k, code % 2, y

        grad_weight += move(piece, owner).astype(F32)

    part = dot(ctx, weight, 1, 1).astype(BF)
    mine = lax.dynamic_slice_in_dim(part, k * 1280, 1280, 1)
    theirs = lax.dynamic_slice_in_dim(part, (1 - k) * 1280, 1280, 1)
    half_sum = (mine.astype(F32) + core_swap(theirs).astype(F32)).astype(BF)
    projected = (half_sum[:384].astype(F32) + x_swap(half_sum[384:]).astype(F32)).astype(BF)

    gc = dot(gout, weight, 1, 0).astype(BF)
    for_a = jnp.where(same, gc[:384], gc[384:])
    for_b = jnp.where(same, gc[384:], gc[:384])
    g_a = move(for_a, lambda z, a, k, l, y: (z, l, k, a, y))
    g_b = move(for_b, lambda z, a, k, l, y: (z, l, k, 1 - a, y))
    grad_context = (g_a.astype(F32) + g_b.astype(F32)).astype(BF)
    return projected, grad_context, grad_weight


def solution(mesh):
    spec = P(("blk", "rep"), "tp")
    return jax.shard_map(
        body,
        mesh=mesh,
        in_specs=(spec, P("blk", "tp"), spec),
        out_specs=(spec, spec, spec),
        check_vma=False,
    )
```

time: 543 us -> 226 us (0.42)
  the two profiles are of different devices: /device:TPU:6 before, /device:TPU:70 now
where the time goes in v1:
time: 226 us; the launch traced here: 225 us
  starting transfers between devices  82.1 us (36%)
  waiting for transfers between devices  81.6 us (36%)
  matrix products  27.8 us (12%)
  between operations  14.5 us (6%)
  other arithmetic  10.6 us (5%)
  local copies, waits for them, and re-layouts  8.67 us (4%)
    ppermute x21, starting transfers between devices, move(): lax.ppermute(value, ALL, [(number(*p), number(*target(*p))) for p in plac...  82 us
    ppermute x21, waiting for transfers between devices, move(): lax.ppermute(value, ALL, [(number(*p), number(*target(*p))) for p in plac...  81.6 us
    dot_general x3, matrix products, dot(): lax.dot_general(a, b, (((ca,), (cb,)), ((), ())), preferred_element_type=...  27.8 us
    unnamed x36, local copies, waits for them, and re-layouts  5.49 us
  transfers between devices with their start and end apart: 22, of which 9 were waited for; matrix products, arithmetic and copies ran while one was open for 18% of the time, Pallas kernels for 0%

profile of v1, /device:TPU:70, one launch (start us, length us, event | category | flops | bytes accessed | tf_op | source)
XLA Modules:
  0.0 225.1 jit_solution(9579084684394504159)
XLA Ops:
  7.2 0.0 all-gather.2.cloned.1.call-start
  7.3 1.1 copy-done
  8.4 7.7 %collective-permute-start.2 = (bf16[320,640]{1,0:T(8,128)(2,1)S(1)}, bf16[320,640]{1,0:T(8,128)(2,1)S(1)}, u32[]{:S(2)}, u32[]{:S(2)}) collective-permute-start(bf16[320,640]{1,0:T(8,128)(2,1)S(1)} %constant_dynamic-slice_fusion.1), channel_id=1, source_target_pairs={{0,0},{1,1},{2,2},{3,3},{4,32},{5,33},{6,34},{7,35},{8,8},{9,9},{1... | collective-permute-start | bytes 1228808 | tf_op jit(solution)/shard_map/ppermute | solution.py:24
  16.0 18.1 %collective-permute-done.2 = bf16[320,640]{1,0:T(8,128)(2,1)S(1)} collective-permute-done((bf16[320,640]{1,0:T(8,128)(2,1)S(1)}, bf16[320,640]{1,0:T(8,128)(2,1)S(1)}, u32[]{:S(2)}, u32[]{:S(2)}) %collective-permute-start.2) | collective-permute-done | bytes 409632 | tf_op jit(solution)/shard_map/ppermute | solution.py:24
  34.1 0.7 copy-done.17
  34.9 2.5 %collective-permute-start.6 = (bf16[384,1280]{1,0:T(8,128)(2,1)}, bf16[384,1280]{1,0:T(8,128)(2,1)S(1)}, u32[]{:S(2)}, u32[]{:S(2)}) collective-permute-start(bf16[384,1280]{1,0:T(8,128)(2,1)} %param.5), channel_id=1, source_target_pairs={{0,4},{1,5},{2,6},{3,7},{4,0},{5,1},{6,2},{7,3},{8,12},{9,13},{10,... | collective-permute-start | bytes 2949128 | tf_op jit(solution)/shard_map/ppermute | solution.py:24
  37.4 1.7 collective-permute-start
  39.1 2.5 %collective-permute-start.1 = (bf16[384,640]{1,0:T(8,128)(2,1)}, bf16[384,640]{1,0:T(8,128)(2,1)}, u32[]{:S(2)}, u32[]{:S(2)}) collective-permute-start(bf16[384,640]{1,0:T(8,128)(2,1)} %param.3), channel_id=1, source_target_pairs={{0,16},{1,17},{2,18},{3,19},{4,0},{5,1},{6,2},{7,3},{8,24},{9,25},... | collective-permute-start | bytes 1474568 | tf_op jit(solution)/shard_map/ppermute | solution.py:24
  41.6 18.7 %collective-permute-done.6 = bf16[384,1280]{1,0:T(8,128)(2,1)S(1)} collective-permute-done((bf16[384,1280]{1,0:T(8,128)(2,1)}, bf16[384,1280]{1,0:T(8,128)(2,1)S(1)}, u32[]{:S(2)}, u32[]{:S(2)}) %collective-permute-start.6) | collective-permute-done | bytes 983072 | tf_op jit(solution)/shard_map/ppermute | solution.py:24
  60.3 8.7 %collective-permute-done.1 = bf16[384,640]{1,0:T(8,128)(2,1)} collective-permute-done((bf16[384,640]{1,0:T(8,128)(2,1)}, bf16[384,640]{1,0:T(8,128)(2,1)}, u32[]{:S(2)}, u32[]{:S(2)}) %collective-permute-start.1) | collective-permute-done | bytes 491552 | tf_op jit(solution)/shard_map/ppermute | solution.py:24
  69.1 1.1 broadcast_select_fusion.7
  70.2 1.7 broadcast_select_fusion.3
  71.9 2.0 broadcast_select_fusion.1
  74.0 16.7 %convolution_convert_fusion.1 = bf16[2560,640]{1,0:T(8,128)(2,1)S(1)} fusion(bf16[384,1280]{1,0:T(8,128)(2,1)S(1)} %get-tuple-element.9, bf16[384,1280]{1,0:T(8,128)(2,1)S(1)} %get-tuple-element.8, bf16[384,1280]{1,0:T(8,128)(2,1)S(1)} %get-tuple-element.7, bf16[384,1280]{1,0:T(8,128)(2,1)S(1)} %get-tuple-element.6, ...), kind=kOutput, calls=%fused_computation.1 | convolution fusion | flops 2535915520 | bytes 8192000 | tf_op jit(solution)/shard_map/dot_general | solution.py:36
  90.8 1.7 copy-done.3
  92.5 1.5 dynamic-slice_bitcast_fusion.2
  94.0 1.6 collective-permute-start.10
  95.6 1.7 collective-permute-start.11
  97.3 2.0 collective-permute-start.12
  99.2 5.9 %convolution_convert_fusion = bf16[768,2560]{1,0:T(8,128)(2,1)S(1)} fusion(bf16[2560,640]{1,0:T(8,128)(2,1)} %all-gather.2.cloned.1.call-done, bf16[384,640]{1,0:T(8,128)(2,1)S(1)} %copy-done.16, bf16[384,640]{1,0:T(8,128)(2,1)S(1)} %copy-done.14), kind=kOutput, calls=%fused_computation | convolution fusion | flops 2520514560 | bytes 8192000 | tf_op jit(solution)/shard_map/dot_general | solution.py:36
  105.2 1.9 copy-done.1
  107.1 1.5 constant_dynamic-slice_fusion
  108.6 7.0 %collective-permute-done.10 = bf16[8,80,640]{2,1,0:T(8,128)(2,1)} collective-permute-done((bf16[8,80,640]{2,1,0:T(8,128)(2,1)}, bf16[8,80,640]{2,1,0:T(8,128)(2,1)}, u32[]{:S(2)}, u32[]{:S(2)}) %collective-permute-start.10) | collective-permute-done | bytes 819232 | tf_op jit(solution)/shard_map/ppermute | solution.py:24
  115.6 1.5 collective-permute-done.11
  117.1 15.6 %collective-permute-done.12 = bf16[8,80,640]{2,1,0:T(8,128)(2,1)} collective-permute-done((bf16[8,80,640]{2,1,0:T(8,128)(2,1)}, bf16[8,80,640]{2,1,0:T(8,128)(2,1)}, u32[]{:S(2)}, u32[]{:S(2)}) %collective-permute-start.12) | collective-permute-done | bytes 819232 | tf_op jit(solution)/shard_map/ppermute | solution.py:24
  132.7 2.3 %fusion.2 = bf16[8,80,640]{2,1,0:T(8,128)(2,1)S(1)} fusion(bf16[8,80,640]{2,1,0:T(8,128)(2,1)} %collective-permute-done.12, bf16[8,80,640]{2,1,0:T(8,128)(2,1)} %collective-permute-done.11, bf16[8,80,640]{2,1,0:T(8,128)(2,1)} %collective-permute-done.10, bf16[8,4,80,640]{3,2,1,0:T(8,128)(2,1)} %bitcast.29, s32[]{:T(128)S(6)} %select_n.166), kind=kLoop, calls=%fused_computation.8 | loop fusion | flops 3276800 | bytes 4096004 | tf_op jit(solution)/shard_map/convert_element_type | solution.py:67
  135.0 0.1 dynamic-slice_bitcast_fusion.10
  135.1 7.8 %collective-permute-start.13 = (bf16[80,640]{1,0:T(8,128)(2,1)S(1)}, bf16[80,640]{1,0:T(8,128)(2,1)S(1)}, u32[]{:S(2)}, u32[]{:S(2)}) collective-permute-start(bf16[80,640]{1,0:T(8,128)(2,1)S(1)} %get-tuple-element.14), channel_id=1, source_target_pairs={{0,0},{1,1},{2,2},{3,3},{4,16},{5,17},{6,18},{7,19},{8,8},{9,9},{1... | collective-permute-start | bytes 307208 | tf_op jit(solution)/shard_map/ppermute | solution.py:24
  142.9 1.9 collective-permute-start.14
  144.8 3.4 %collective-permute-start.15 = (bf16[80,640]{1,0:T(8,128)(2,1)S(1)}, bf16[80,640]{1,0:T(8,128)(2,1)S(1)}, u32[]{:S(2)}, u32[]{:S(2)}) collective-permute-start(bf16[80,640]{1,0:T(8,128)(2,1)S(1)} %get-tuple-element.20), channel_id=1, source_target_pairs={{0,32},{1,33},{2,34},{3,35},{4,48},{5,49},{6,50},{7,51},{8,40},{9,... | collective-permute-start | bytes 307208 | tf_op jit(solution)/shard_map/ppermute | solution.py:24
  148.3 4.8 %collective-permute-start.16 = (bf16[80,640]{1,0:T(8,128)(2,1)S(1)}, bf16[80,640]{1,0:T(8,128)(2,1)S(1)}, u32[]{:S(2)}, u32[]{:S(2)}) collective-permute-start(bf16[80,640]{1,0:T(8,128)(2,1)S(1)} %get-tuple-element.19), channel_id=1, source_target_pairs={{0,36},{1,37},{2,38},{3,39},{4,52},{5,53},{6,54},{7,55},{8,44},{9,... | collective-permute-start | bytes 307208 | tf_op jit(solution)/shard_map/ppermute | solution.py:24
  153.1 5.1 %convolution_convert_fusion.2 = bf16[768,640]{1,0:T(8,128)(2,1)S(1)} fusion(bf16[2560,640]{1,0:T(8,128)(2,1)} %all-gather.2.cloned.1.call-done, bf16[384,1280]{1,0:T(8,128)(2,1)S(1)} %copy-done.12, bf16[384,1280]{1,0:T(8,128)(2,1)S(1)} %copy-done.10, bf16[384,1280]{1,0:T(8,128)(2,1)S(1)} %copy-done.8, bf16[384,1280]{1,0:T(8,128)(2,1)S(1)} %copy-done.6), kind=kOutput, calls=%fused_computation.9 | convolution fusion | flops 2532802560 | bytes 8192000 | tf_op jit(solution)/shard_map/dot_general | solution.py:36
  158.3 0.5 add_convert_fusion
  158.8 0.1 slice.19
  158.9 2.9 %collective-permute-start.4 = (bf16[384,1280]{1,0:T(8,128)(2,1)S(1)}, bf16[384,1280]{1,0:T(8,128)(2,1)S(1)}, u32[]{:S(2)}, u32[]{:S(2)}) collective-permute-start(bf16[384,1280]{1,0:T(8,128)(2,1)S(1)} %slice.19), channel_id=1, source_target_pairs={{0,4},{1,5},{2,6},{3,7},{4,0},{5,1},{6,2},{7,3},{8,12},{9,13},{10,... | collective-permute-start | bytes 2949128 | tf_op jit(solution)/shard_map/ppermute | solution.py:24
  161.7 0.1 broadcast_select_fusion.5
  161.8 0.7 collective-permute-start.8
  162.6 1.3 collective-permute-start.9
  163.9 4.6 %collective-permute-start.17 = (bf16[80,640]{1,0:T(8,128)(2,1)S(1)}, bf16[80,640]{1,0:T(8,128)(2,1)S(1)}, u32[]{:S(2)}, u32[]{:S(2)}) collective-permute-start(bf16[80,640]{1,0:T(8,128)(2,1)S(1)} %get-tuple-element.18), channel_id=1, source_target_pairs={{0,64},{1,65},{2,66},{3,67},{4,80},{5,81},{6,82},{7,83},{8,72},{9,... | collective-permute-start | bytes 307208 | tf_op jit(solution)/shard_map/ppermute | solution.py:24
  168.4 3.4 %collective-permute-start.18 = (bf16[80,640]{1,0:T(8,128)(2,1)S(1)}, bf16[80,640]{1,0:T(8,128)(2,1)S(1)}, u32[]{:S(2)}, u32[]{:S(2)}) collective-permute-start(bf16[80,640]{1,0:T(8,128)(2,1)S(1)} %get-tuple-element.17), channel_id=1, source_target_pairs={{0,68},{1,69},{2,70},{3,71},{4,84},{5,85},{6,86},{7,87},{8,76},{9,... | collective-permute-start | bytes 307208 | tf_op jit(solution)/shard_map/ppermute | solution.py:24
  171.8 0.9 collective-permute-done.17
  172.8 29.8 %collective-permute-start.19 = (bf16[80,640]{1,0:T(8,128)(2,1)S(1)}, bf16[80,640]{1,0:T(8,128)(2,1)S(1)}, u32[]{:S(2)}, u32[]{:S(2)}) collective-permute-start(bf16[80,640]{1,0:T(8,128)(2,1)S(1)} %get-tuple-element.16), channel_id=1, source_target_pairs={{0,96},{1,97},{2,98},{3,99},{4,112},{5,113},{6,114},{7,115},{8,104... | collective-permute-start | bytes 307208 | tf_op jit(solution)/shard_map/ppermute | solution.py:24
  202.5 1.9 collective-permute-start.20
  204.5 0.3 collective-permute-done.19
  204.8 10.6 %collective-permute-done.20 = bf16[80,640]{1,0:T(8,128)(2,1)S(1)} collective-permute-done((bf16[80,640]{1,0:T(8,128)(2,1)S(1)}, bf16[80,640]{1,0:T(8,128)(2,1)S(1)}, u32[]{:S(2)}, u32[]{:S(2)}) %collective-permute-start.20) | collective-permute-done | bytes 102432 | tf_op jit(solution)/shard_map/ppermute | solution.py:24
  215.4 0.8 convert_add_fusion.1
  216.2 0.9 add_convert_fusion.2
  217.1 1.2 add_convert_fusion.1
  (50 shorter events, 0.2 us)
Async XLA Ops:
  7.2 1.2 copy-start
  7.2 63.1 %copy-start.4 = (bf16[384,1280]{1,0:T(8,128)(2,1)S(1)}, bf16[384,1280]{1,0:T(8,128)(2,1)}, u32[]{:S(2)}) copy-start(bf16[384,1280]{1,0:T(8,128)(2,1)} %param.5) | copy-start | bytes 2949124
  7.2 92.1 %all-gather.2.cloned.1.call-start = ((), (), s32[]{:S(2)}) async-start(), calls=%async_computation | async-start | bytes 3686400 | tf_op jit(solution)/shard_map/all_gather | solution.py:47
  8.4 25.8 %collective-permute-start.2 = (bf16[320,640]{1,0:T(8,128)(2,1)S(1)}, bf16[320,640]{1,0:T(8,128)(2,1)S(1)}, u32[]{:S(2)}, u32[]{:S(2)}) collective-permute-start(bf16[320,640]{1,0:T(8,128)(2,1)S(1)} %constant_dynamic-slice_fusion.1), channel_id=1, source_target_pairs={{0,0},{1,1},{2,2},{3,3},{4,32},{5,33},{6,34},{7,35},{8,8},{9,9},{1... | collective-permute-start | bytes 1228808 | tf_op jit(solution)/shard_map/ppermute | solution.py:24
  34.1 0.7 copy-start.17
  34.9 25.4 %collective-permute-start.6 = (bf16[384,1280]{1,0:T(8,128)(2,1)}, bf16[384,1280]{1,0:T(8,128)(2,1)S(1)}, u32[]{:S(2)}, u32[]{:S(2)}) collective-permute-start(bf16[384,1280]{1,0:T(8,128)(2,1)} %param.5), channel_id=1, source_target_pairs={{0,4},{1,5},{2,6},{3,7},{4,0},{5,1},{6,2},{7,3},{8,12},{9,13},{10,... | collective-permute-start | bytes 2949128 | tf_op jit(solution)/shard_map/ppermute | solution.py:24
  37.4 32.8 %collective-permute-start.5 = (bf16[384,1280]{1,0:T(8,128)(2,1)}, bf16[384,1280]{1,0:T(8,128)(2,1)}, u32[]{:S(2)}, u32[]{:S(2)}) collective-permute-start(bf16[384,1280]{1,0:T(8,128)(2,1)} %param.5), channel_id=1, source_target_pairs={{0,8},{1,9},{2,10},{3,11},{4,12},{5,13},{6,14},{7,15},{8,0},{9,1},... | collective-permute-start | bytes 2949128 | tf_op jit(solution)/shard_map/ppermute | solution.py:24
  37.4 22.9 %collective-permute-start = (bf16[384,640]{1,0:T(8,128)(2,1)}, bf16[384,640]{1,0:T(8,128)(2,1)S(1)}, u32[]{:S(2)}, u32[]{:S(2)}) collective-permute-start(bf16[384,640]{1,0:T(8,128)(2,1)} %param.3), channel_id=1, source_target_pairs={{0,0},{1,1},{2,2},{3,3},{4,16},{5,17},{6,18},{7,19},{8,8},{9,9},{1... | collective-permute-start | bytes 1474568 | tf_op jit(solution)/shard_map/ppermute | solution.py:24
  39.1 29.9 %collective-permute-start.1 = (bf16[384,640]{1,0:T(8,128)(2,1)}, bf16[384,640]{1,0:T(8,128)(2,1)}, u32[]{:S(2)}, u32[]{:S(2)}) collective-permute-start(bf16[384,640]{1,0:T(8,128)(2,1)} %param.3), channel_id=1, source_target_pairs={{0,16},{1,17},{2,18},{3,19},{4,0},{5,1},{6,2},{7,3},{8,24},{9,25},... | collective-permute-start | bytes 1474568 | tf_op jit(solution)/shard_map/ppermute | solution.py:24
  60.3 11.6 %collective-permute-start.7 = (bf16[384,1280]{1,0:T(8,128)(2,1)S(1)}, bf16[384,1280]{1,0:T(8,128)(2,1)}, u32[]{:S(2)}, u32[]{:S(2)}) collective-permute-start(bf16[384,1280]{1,0:T(8,128)(2,1)S(1)} %collective-permute-done.6), channel_id=1, source_target_pairs={{0,8},{1,9},{2,10},{3,11},{4,12},{5,13},{6,14},{7,15},{8,0},{9,1},... | collective-permute-start | bytes 2949128 | tf_op jit(solution)/shard_map/ppermute | solution.py:24
  70.2 3.8 %copy-start.13 = (bf16[384,640]{1,0:T(8,128)(2,1)}, bf16[384,640]{1,0:T(8,128)(2,1)S(1)}, u32[]{:S(2)}) copy-start(bf16[384,640]{1,0:T(8,128)(2,1)S(1)} %get-tuple-element.12) | copy-start | bytes 1474564
  70.2 3.8 %copy-start.15 = (bf16[384,640]{1,0:T(8,128)(2,1)}, bf16[384,640]{1,0:T(8,128)(2,1)S(1)}, u32[]{:S(2)}) copy-start(bf16[384,640]{1,0:T(8,128)(2,1)S(1)} %get-tuple-element.13) | copy-start | bytes 1474564
  71.9 18.8 %copy-start.5 = (bf16[384,1280]{1,0:T(8,128)(2,1)}, bf16[384,1280]{1,0:T(8,128)(2,1)S(1)}, u32[]{:S(2)}) copy-start(bf16[384,1280]{1,0:T(8,128)(2,1)S(1)} %get-tuple-element.6) | copy-start | bytes 2949124
  71.9 18.8 %copy-start.7 = (bf16[384,1280]{1,0:T(8,128)(2,1)}, bf16[384,1280]{1,0:T(8,128)(2,1)S(1)}, u32[]{:S(2)}) copy-start(bf16[384,1280]{1,0:T(8,128)(2,1)S(1)} %get-tuple-element.7) | copy-start | bytes 2949124
  74.0 16.7 %copy-start.9 = (bf16[384,1280]{1,0:T(8,128)(2,1)}, bf16[384,1280]{1,0:T(8,128)(2,1)S(1)}, u32[]{:S(2)}) copy-start(bf16[384,1280]{1,0:T(8,128)(2,1)S(1)} %get-tuple-element.8) | copy-start | bytes 2949124
  74.0 16.7 %copy-start.11 = (bf16[384,1280]{1,0:T(8,128)(2,1)}, bf16[384,1280]{1,0:T(8,128)(2,1)S(1)}, u32[]{:S(2)}) copy-start(bf16[384,1280]{1,0:T(8,128)(2,1)S(1)} %get-tuple-element.9) | copy-start | bytes 2949124
  90.7 1.8 copy-start.3
  90.7 8.5 %copy-start.14 = (bf16[384,640]{1,0:T(8,128)(2,1)S(1)}, bf16[384,640]{1,0:T(8,128)(2,1)}, u32[]{:S(2)}) copy-start(bf16[384,640]{1,0:T(8,128)(2,1)} %copy-done.13) | copy-start | bytes 1474564
  90.7 8.5 %copy-start.16 = (bf16[384,640]{1,0:T(8,128)(2,1)S(1)}, bf16[384,640]{1,0:T(8,128)(2,1)}, u32[]{:S(2)}) copy-start(bf16[384,640]{1,0:T(8,128)(2,1)} %copy-done.15) | copy-start | bytes 1474564
  94.0 21.6 %collective-permute-start.10 = (bf16[8,80,640]{2,1,0:T(8,128)(2,1)}, bf16[8,80,640]{2,1,0:T(8,128)(2,1)}, u32[]{:S(2)}, u32[]{:S(2)}) collective-permute-start(bf16[8,80,640]{2,1,0:T(8,128)(2,1)} %get-tuple-element.3), channel_id=1, source_target_pairs={{0,1},{1,2},{2,3},{3,0},{4,5},{5,6},{6,7},{7,4},{8,9},{9,10},{10,1... | collective-permute-start | bytes 2457608 | tf_op jit(solution)/shard_map/ppermute | solution.py:24
  95.6 21.5 %collective-permute-start.11 = (bf16[8,80,640]{2,1,0:T(8,128)(2,1)}, bf16[8,80,640]{2,1,0:T(8,128)(2,1)}, u32[]{:S(2)}, u32[]{:S(2)}) collective-permute-start(bf16[8,80,640]{2,1,0:T(8,128)(2,1)} %get-tuple-element.5), channel_id=1, source_target_pairs={{0,3},{1,0},{2,1},{3,2},{4,7},{5,4},{6,5},{7,6},{8,11},{9,8},{10,9... | collective-permute-start | bytes 2457608 | tf_op jit(solution)/shard_map/ppermute | solution.py:24
  97.3 35.5 %collective-permute-start.12 = (bf16[8,80,640]{2,1,0:T(8,128)(2,1)}, bf16[8,80,640]{2,1,0:T(8,128)(2,1)}, u32[]{:S(2)}, u32[]{:S(2)}) collective-permute-start(bf16[8,80,640]{2,1,0:T(8,128)(2,1)} %get-tuple-element.4), channel_id=1, source_target_pairs={{0,2},{1,3},{2,0},{3,1},{4,6},{5,7},{6,4},{7,5},{8,10},{9,11},{10,... | collective-permute-start | bytes 2457608 | tf_op jit(solution)/shard_map/ppermute | solution.py:24
  105.2 1.9 copy-start.1
  108.5 49.7 %collective-permute-start.3 = (bf16[768,1280]{1,0:T(8,128)(2,1)}, bf16[768,1280]{1,0:T(8,128)(2,1)S(1)}, u32[]{:S(2)}, u32[]{:S(2)}) collective-permute-start(bf16[768,1280]{1,0:T(8,128)(2,1)} %constant_dynamic-slice_fusion), channel_id=1, source_target_pairs={{0,8},{1,9},{2,10},{3,11},{4,12},{5,13},{6,14},{7,15},{8,0},{9,1},... | collective-permute-start | bytes 5898248 | tf_op jit(solution)/shard_map/ppermute | solution.py:24
  108.5 44.5 %copy-start.6 = (bf16[384,1280]{1,0:T(8,128)(2,1)S(1)}, bf16[384,1280]{1,0:T(8,128)(2,1)}, u32[]{:S(2)}) copy-start(bf16[384,1280]{1,0:T(8,128)(2,1)} %copy-done.5) | copy-start | bytes 2949124
  108.5 44.5 %copy-start.8 = (bf16[384,1280]{1,0:T(8,128)(2,1)S(1)}, bf16[384,1280]{1,0:T(8,128)(2,1)}, u32[]{:S(2)}) copy-start(bf16[384,1280]{1,0:T(8,128)(2,1)} %copy-done.7) | copy-start | bytes 2949124
  108.5 44.5 %copy-start.10 = (bf16[384,1280]{1,0:T(8,128)(2,1)S(1)}, bf16[384,1280]{1,0:T(8,128)(2,1)}, u32[]{:S(2)}) copy-start(bf16[384,1280]{1,0:T(8,128)(2,1)} %copy-done.9) | copy-start | bytes 2949124
  108.6 44.5 %copy-start.12 = (bf16[384,1280]{1,0:T(8,128)(2,1)S(1)}, bf16[384,1280]{1,0:T(8,128)(2,1)}, u32[]{:S(2)}) copy-start(bf16[384,1280]{1,0:T(8,128)(2,1)} %copy-done.11) | copy-start | bytes 2949124
  135.1 26.7 %collective-permute-start.13 = (bf16[80,640]{1,0:T(8,128)(2,1)S(1)}, bf16[80,640]{1,0:T(8,128)(2,1)S(1)}, u32[]{:S(2)}, u32[]{:S(2)}) collective-permute-start(bf16[80,640]{1,0:T(8,128)(2,1)S(1)} %get-tuple-element.14), channel_id=1, source_target_pairs={{0,0},{1,1},{2,2},{3,3},{4,16},{5,17},{6,18},{7,19},{8,8},{9,9},{1... | collective-permute-start | bytes 307208 | tf_op jit(solution)/shard_map/ppermute | solution.py:24
  142.9 19.7 %collective-permute-start.14 = (bf16[80,640]{1,0:T(8,128)(2,1)S(1)}, bf16[80,640]{1,0:T(8,128)(2,1)S(1)}, u32[]{:S(2)}, u32[]{:S(2)}) collective-permute-start(bf16[80,640]{1,0:T(8,128)(2,1)S(1)} %get-tuple-element.21), channel_id=1, source_target_pairs={{0,4},{1,5},{2,6},{3,7},{4,20},{5,21},{6,22},{7,23},{8,12},{9,13},... | collective-permute-start | bytes 307208 | tf_op jit(solution)/shard_map/ppermute | solution.py:24
  144.8 19.1 %collective-permute-start.15 = (bf16[80,640]{1,0:T(8,128)(2,1)S(1)}, bf16[80,640]{1,0:T(8,128)(2,1)S(1)}, u32[]{:S(2)}, u32[]{:S(2)}) collective-permute-start(bf16[80,640]{1,0:T(8,128)(2,1)S(1)} %get-tuple-element.20), channel_id=1, source_target_pairs={{0,32},{1,33},{2,34},{3,35},{4,48},{5,49},{6,50},{7,51},{8,40},{9,... | collective-permute-start | bytes 307208 | tf_op jit(solution)/shard_map/ppermute | solution.py:24
  148.2 10.0 %copy-start.2 = (bf16[768,2560]{1,0:T(8,128)(2,1)S(1)}, bf16[768,2560]{1,0:T(8,128)(2,1)}, u32[]{:S(2)}) copy-start(bf16[768,2560]{1,0:T(8,128)(2,1)} %copy-done.1) | copy-start | bytes 11796484
  148.3 20.2 %collective-permute-start.16 = (bf16[80,640]{1,0:T(8,128)(2,1)S(1)}, bf16[80,640]{1,0:T(8,128)(2,1)S(1)}, u32[]{:S(2)}, u32[]{:S(2)}) collective-permute-start(bf16[80,640]{1,0:T(8,128)(2,1)S(1)} %get-tuple-element.19), channel_id=1, source_target_pairs={{0,36},{1,37},{2,38},{3,39},{4,52},{5,53},{6,54},{7,55},{8,44},{9,... | collective-permute-start | bytes 307208 | tf_op jit(solution)/shard_map/ppermute | solution.py:24
  158.9 58.2 %collective-permute-start.4 = (bf16[384,1280]{1,0:T(8,128)(2,1)S(1)}, bf16[384,1280]{1,0:T(8,128)(2,1)S(1)}, u32[]{:S(2)}, u32[]{:S(2)}) collective-permute-start(bf16[384,1280]{1,0:T(8,128)(2,1)S(1)} %slice.19), channel_id=1, source_target_pairs={{0,4},{1,5},{2,6},{3,7},{4,0},{5,1},{6,2},{7,3},{8,12},{9,13},{10,... | collective-permute-start | bytes 2949128 | tf_op jit(solution)/shard_map/ppermute | solution.py:24
  161.8 54.4 %collective-permute-start.8 = (bf16[384,640]{1,0:T(8,128)(2,1)S(1)}, bf16[384,640]{1,0:T(8,128)(2,1)S(1)}, u32[]{:S(2)}, u32[]{:S(2)}) collective-permute-start(bf16[384,640]{1,0:T(8,128)(2,1)S(1)} %get-tuple-element.10), channel_id=1, source_target_pairs={{0,0},{1,1},{2,2},{3,3},{4,16},{5,17},{6,18},{7,19},{8,8},{9,9},{1... | collective-permute-start | bytes 1474568 | tf_op jit(solution)/shard_map/ppermute | solution.py:24
  162.6 53.7 %collective-permute-start.9 = (bf16[384,640]{1,0:T(8,128)(2,1)S(1)}, bf16[384,640]{1,0:T(8,128)(2,1)S(1)}, u32[]{:S(2)}, u32[]{:S(2)}) collective-permute-start(bf16[384,640]{1,0:T(8,128)(2,1)S(1)} %get-tuple-element.11), channel_id=1, source_target_pairs={{0,4},{1,5},{2,6},{3,7},{4,20},{5,21},{6,22},{7,23},{8,12},{9,13},... | collective-permute-start | bytes 1474568 | tf_op jit(solution)/shard_map/ppermute | solution.py:24
  163.9 8.9 %collective-permute-start.17 = (bf16[80,640]{1,0:T(8,128)(2,1)S(1)}, bf16[80,640]{1,0:T(8,128)(2,1)S(1)}, u32[]{:S(2)}, u32[]{:S(2)}) collective-permute-start(bf16[80,640]{1,0:T(8,128)(2,1)S(1)} %get-tuple-element.18), channel_id=1, source_target_pairs={{0,64},{1,65},{2,66},{3,67},{4,80},{5,81},{6,82},{7,83},{8,72},{9,... | collective-permute-start | bytes 307208 | tf_op jit(solution)/shard_map/ppermute | solution.py:24
  168.4 34.1 %collective-permute-start.18 = (bf16[80,640]{1,0:T(8,128)(2,1)S(1)}, bf16[80,640]{1,0:T(8,128)(2,1)S(1)}, u32[]{:S(2)}, u32[]{:S(2)}) collective-permute-start(bf16[80,640]{1,0:T(8,128)(2,1)S(1)} %get-tuple-element.17), channel_id=1, source_target_pairs={{0,68},{1,69},{2,70},{3,71},{4,84},{5,85},{6,86},{7,87},{8,76},{9,... | collective-permute-start | bytes 307208 | tf_op jit(solution)/shard_map/ppermute | solution.py:24
  172.8 32.0 %collective-permute-start.19 = (bf16[80,640]{1,0:T(8,128)(2,1)S(1)}, bf16[80,640]{1,0:T(8,128)(2,1)S(1)}, u32[]{:S(2)}, u32[]{:S(2)}) collective-permute-start(bf16[80,640]{1,0:T(8,128)(2,1)S(1)} %get-tuple-element.16), channel_id=1, source_target_pairs={{0,96},{1,97},{2,98},{3,99},{4,112},{5,113},{6,114},{7,115},{8,104... | collective-permute-start | bytes 307208 | tf_op jit(solution)/shard_map/ppermute | solution.py:24
  202.5 12.9 %collective-permute-start.20 = (bf16[80,640]{1,0:T(8,128)(2,1)S(1)}, bf16[80,640]{1,0:T(8,128)(2,1)S(1)}, u32[]{:S(2)}, u32[]{:S(2)}) collective-permute-start(bf16[80,640]{1,0:T(8,128)(2,1)S(1)} %get-tuple-element.15), channel_id=1, source_target_pairs={{0,100},{1,101},{2,102},{3,103},{4,116},{5,117},{6,118},{7,119},{8... | collective-permute-start | bytes 307208 | tf_op jit(solution)/shard_map/ppermute | solution.py:24
Sparse Core Ops, SparseCore 0:
  35.0 46.4 all-gather.1

commit v2 on v1

v2 whole, which is shorter than its diff:
```python
import functools

import jax
import jax.numpy as jnp
from jax import lax
from jax.experimental import pallas as pl
from jax.experimental.pallas import tpu as pltpu
from jax.sharding import PartitionSpec as P

BF, F32 = jnp.bfloat16, jnp.float32
ALL = ("blk", "tp", "rep")


def number(z, a, k, l, y):
    return (z * 4 + a * 2 + k) * 8 + l * 4 + y


def places():
    for z in range(8):
        for a in range(2):
            for k in range(2):
                for l in range(2):
                    for y in range(4):
                        yield z, a, k, l, y


def move(value, target):
    pairs = [(number(*p), number(*target(*p))) for p in places() if target(*p)]
    return lax.ppermute(value, ALL, pairs)


def swap_core(v):
    return move(v, lambda z, a, k, l, y: (z, a, 1 - k, l, y))


def swap_lo(v):
    return move(v, lambda z, a, k, l, y: (z, a, k, 1 - l, y))


def swap_hi(v):
    return move(v, lambda z, a, k, l, y: (z, 1 - a, k, l, y))


def swap_both(v):
    return move(v, lambda z, a, k, l, y: (z, 1 - a, k, 1 - l, y))


def to_pair(z, a, k, l, y):
    return (z ^ 1, a, k, l, y) if z % 2 == l else None


def to_home(z, a, k, l, y):
    return (z - z % 2 + l, a, k, z % 2, y)


def dot(a, b, ca, cb):
    return lax.dot_general(a, b, (((ca,), (cb,)), ((), ())), preferred_element_type=F32)


def add(*terms):
    total = terms[0].astype(F32)
    for term in terms[1:]:
        total = total + term.astype(F32)
    return total


def pick(v, i, axis):
    return lax.dynamic_index_in_dim(v, i, axis, keepdims=False)


def over_y(v, y):
    axis = v.ndim - 3
    got = [pick(v, y, axis)]
    for d in (1, 3, 2):
        got.append(move(pick(v, (y + d) % 4, axis), lambda z, a, k, l, y: (z, a, k, l, (y + d) % 4)))
    return add(*got)


def call(kernel, outs, flops, n_in):
    whole = pl.BlockSpec(memory_space=pltpu.VMEM)
    return pl.pallas_call(
        kernel,
        out_shape=[jax.ShapeDtypeStruct(s, BF) for s in outs],
        in_specs=[pl.BlockSpec(memory_space=pltpu.SMEM)] + [whole] * n_in,
        out_specs=[whole] * len(outs),
        compiler_params=pltpu.CompilerParams(vmem_limit_bytes=40 << 20),
        cost_estimate=pl.CostEstimate(flops=flops, bytes_accessed=8 << 20, transcendentals=0),
    )


WORK = 2 * 768 * 2560 * 640


def gw_kernel(t, *refs):
    g_own, g_far, c_own, c_far, out = refs[:4], refs[4:8], refs[8], refs[9], refs[10]
    for q in range(4):
        out[t[0] ^ q] = (dot(g_own[q][...], c_own[...], 0, 0) + dot(g_far[q][...], c_far[...], 0, 0)).astype(BF)


def proj_kernel(t, c_own, c_far, w, *outs):
    for q in (1, 3, 0, 2):
        for s, c in enumerate((c_far, c_own)):
            outs[q % 2][q // 2, s] = dot(c[...], w[t[0] ^ q], 1, 1).astype(BF)


def gc_kernel(t, *refs):
    w, far, own = refs[8:]
    for g, out in ((refs[4:8], far), (refs[:4], own)):
        total = dot(g[0][...], w[t[0]], 1, 0)
        for q in range(1, 4):
            total += dot(g[q][...], w[t[0] ^ q], 1, 0)
        out[...] = total.astype(BF)


def body(context, out_weight, grad_out):
    z = lax.axis_index("blk")
    t = lax.axis_index("tp")
    r = lax.axis_index("rep")
    f, y = r // 4, r % 4
    at = t.astype(jnp.int32).reshape(1)

    part = lax.dynamic_slice_in_dim(out_weight, (1 - f) * 320, 320, 0)
    mine = lax.dynamic_slice_in_dim(out_weight, f * 320, 320, 0)
    part = jnp.where(z % 2 == f, mine, move(part, to_pair))
    weight = lax.all_gather(part, "blk", axis=0, tiled=True)

    g_mine = lax.dynamic_slice_in_dim(grad_out, f * 640, 640, 1)
    g_theirs = lax.dynamic_slice_in_dim(grad_out, (1 - f) * 640, 640, 1)
    near = swap_lo(g_theirs)
    c_far = swap_lo(context)
    cross = swap_both(g_theirs)
    hi = swap_hi(g_mine)
    own = [g_mine, swap_core(g_mine), hi, swap_core(hi)]
    far = [near, swap_core(near), cross, swap_core(cross)]

    gw = call(gw_kernel, [(4, 640, 640)], WORK, 10)(at, *own, *far, context, c_far)[0]
    gw, weight = lax.optimization_barrier((gw, weight))
    gw = lax.psum_scatter(gw.reshape(8, 4, 80, 640), "blk", scatter_dimension=0, tiled=True)
    grad_weight = move(over_y(gw[0], y).astype(BF), to_home).astype(F32)

    w = weight.reshape(4, 640, 640)
    keep, give = call(proj_kernel, [(2, 2, 384, 640)] * 2, WORK, 3)(at, context, c_far, w)
    keep = add(keep, swap_core(give)).astype(BF)
    first = add(keep[0, 1], swap_hi(keep[1, 1])).astype(BF)
    second = add(swap_lo(keep[0, 0]), swap_both(keep[1, 0])).astype(BF)
    low = f == 0
    projected = jnp.concatenate([jnp.where(low, first, second), jnp.where(low, second, first)], axis=1)

    gc_far, gc_own = call(gc_kernel, [(384, 640)] * 2, WORK, 9)(at, *own, *far, w)
    grad_context = add(gc_own, swap_lo(gc_far)).astype(BF)
    return projected, grad_context, grad_weight


def solution(mesh):
    spec = P(("blk", "rep"), "tp")
    return jax.shard_map(
        body,
        mesh=mesh,
        in_specs=(spec, P("blk", "tp"), spec),
        out_specs=(spec, spec, spec),
        check_vma=False,
    )
```

time: 226 us -> 148 us (0.65)
  the two profiles are of different devices: /device:TPU:70 before, /device:TPU:6 now
where the time goes in v2:
time: 148 us
  waiting for transfers between devices  83.1 us (56%)
  starting transfers between devices  19.4 us (13%)
  Pallas kernels  17 us (11%)
  between operations  14.2 us (10%)
  other arithmetic  8.43 us (6%)
  local copies, waits for them, and re-layouts  5.33 us (4%)
    ppermute x18, waiting for transfers between devices, move(): return lax.ppermute(value, ALL, pairs)  53.3 us
    reduce_scatter x1, waiting for transfers between devices, body(): lax.psum_scatter(gw.reshape(8, 4, 80, 640), 'blk', scatter_dimension=0, t...  20.3 us
    ppermute x18, starting transfers between devices, move(): return lax.ppermute(value, ALL, pairs)  19.4 us
    all_gather x1, waiting for transfers between devices, body(): weight = lax.all_gather(part, 'blk', axis=0, tiled=True)  9.47 us
    pallas_call x1, Pallas kernels, body(): call(gw_kernel, [(4, 640, 640)], WORK, 10)(at, *own, *far, context, c_far)  7.14 us
    pallas_call x1, Pallas kernels, body(): call(proj_kernel, [(2, 2, 384, 640)] * 2, WORK, 3)(at, context, c_far, w)  4.99 us
    pallas_call x1, Pallas kernels, body(): call(gc_kernel, [(384, 640)] * 2, WORK, 9)(at, *own, *far, w)  4.86 us
  transfers between devices with their start and end apart: 20, of which 11 were waited for; matrix products, arithmetic and copies ran while one was open for 5% of the time, Pallas kernels for 12%

profile of v2, /device:TPU:6, one launch (start us, length us, event | category | flops | bytes accessed | tf_op | source)
XLA Modules:
  0.0 147.5 jit_solution(5976271977328541372)
XLA Ops:
  7.2 0.0 all-gather.2.cloned.1.call-start
  7.2 1.1 constant_dynamic-slice_fusion
  8.4 0.0 copy-start.2
  8.4 1.4 collective-permute-start.8
  9.8 11.8 %collective-permute-done.8 = bf16[320,640]{1,0:T(8,128)(2,1)S(1)} collective-permute-done((bf16[320,640]{1,0:T(8,128)(2,1)S(1)}, bf16[320,640]{1,0:T(8,128)(2,1)S(1)}, u32[]{:S(2)}, u32[]{:S(2)}) %collective-permute-start.8) | collective-permute-done | bytes 409632 | tf_op jit(solution)/shard_map/ppermute | solution.py:29
  21.6 1.9 %dynamic-slice_select_fusion = bf16[320,640]{1,0:T(8,128)(2,1)} fusion(bf16[320,640]{1,0:T(8,128)(2,1)S(1)} %collective-permute-done.8, bf16[640,640]{1,0:T(8,128)(2,1)} %param.4, s32[]{:T(128)S(6)} %select_n.78, pred[]{:T(512)S(6)} %eq.13), kind=kLoop, calls=%fused_computation.12 | loop fusion | flops 204800 | bytes 1228805 | tf_op jit(solution)/shard_map/jit(_where)/select_n | solution.py:124
  23.5 0.0 all-gather.2.cloned.1.call-update
  23.5 0.0 reduce-scatter.2.cloned.1.call-start
  23.5 0.1 constant_dynamic-slice_fusion.1
  23.6 1.5 %collective-permute-start.2 = (bf16[384,640]{1,0:T(8,128)(2,1)S(1)}, bf16[384,640]{1,0:T(8,128)(2,1)S(1)}, u32[]{:S(2)}, u32[]{:S(2)}) collective-permute-start(bf16[384,640]{1,0:T(8,128)(2,1)S(1)} %get-tuple-element.21.refs_0_), channel_id=1, source_target_pairs={{0,16},{1,17},{2,18},{3,19},{4,20},{5,21},{6,22},{7,23},{8,24},{9,... | collective-permute-start | bytes 1474568 | tf_op jit(solution)/shard_map/ppermute | solution.py:29
  25.1 2.7 %collective-permute-start.6 = (bf16[384,640]{1,0:T(8,128)(2,1)S(1)}, bf16[384,640]{1,0:T(8,128)(2,1)S(1)}, u32[]{:S(2)}, u32[]{:S(2)}) collective-permute-start(bf16[384,640]{1,0:T(8,128)(2,1)S(1)} %get-tuple-element.20), channel_id=1, source_target_pairs={{0,20},{1,21},{2,22},{3,23},{4,16},{5,17},{6,18},{7,19},{8,28},{9,... | collective-permute-start | bytes 1474568 | tf_op jit(solution)/shard_map/ppermute | solution.py:29
  27.8 0.0 collective-permute-start.1
  27.8 0.3 collective-permute-start
  28.1 11.3 %collective-permute-done.2.refs_2_ = bf16[384,640]{1,0:T(8,128)(2,1)S(1)} collective-permute-done((bf16[384,640]{1,0:T(8,128)(2,1)S(1)}, bf16[384,640]{1,0:T(8,128)(2,1)S(1)}, u32[]{:S(2)}, u32[]{:S(2)}) %collective-permute-start.2) | collective-permute-done | bytes 491552 | tf_op jit(solution)/shard_map/ppermute | solution.py:29
  39.4 0.0 collective-permute-start.3
  39.4 7.9 %collective-permute-done.4.refs_4_ = bf16[384,640]{1,0:T(8,128)(2,1)S(1)} collective-permute-done((bf16[384,640]{1,0:T(8,128)(2,1)S(1)}, bf16[384,640]{1,0:T(8,128)(2,1)S(1)}, u32[]{:S(2)}, u32[]{:S(2)}) %collective-permute-start.4) | collective-permute-done | bytes 491552 | tf_op jit(solution)/shard_map/ppermute | solution.py:29
  47.4 0.0 collective-permute-start.5
  47.4 0.5 collective-permute-done.6.refs_6_
  47.9 0.1 collective-permute-start.7
  48.0 7.9 %collective-permute-done.refs_9_.c_far = bf16[384,640]{1,0:T(8,128)(2,1)} collective-permute-done((bf16[384,640]{1,0:T(8,128)(2,1)S(1)}, bf16[384,640]{1,0:T(8,128)(2,1)}, u32[]{:S(2)}, u32[]{:S(2)}) %collective-permute-start) | collective-permute-done | bytes 491552 | tf_op jit(solution)/shard_map/ppermute | solution.py:29
  55.9 7.1 %shard_map.58 = bf16[4,640,640]{2,1,0:T(8,128)(2,1)} custom-call(s32[1]{0:T(128)} %bitcast.t, bf16[384,640]{1,0:T(8,128)(2,1)S(1)} %get-tuple-element.21.refs_0_, bf16[384,640]{1,0:T(8,128)(2,1)S(1)} %collective-permute-done.1.refs_1_, bf16[384,640]{1,0:T(8,128)(2,1)S(1)} %collective-permute-done.2.refs_2_, ...), custom_call_target="tpu_custom_call" | custom-call | flops 2516582400 | bytes 8388608 | tf_op jit(solution)/shard_map/pallas_call | solution.py:136
  63.0 9.5 %all-gather.2.cloned.1.call-done = bf16[2560,640]{1,0:T(8,128)(2,1)} async-done(((bf16[320,640]{1,0:T(8,128)(2,1)}), bf16[2560,640]{1,0:T(8,128)(2,1)}) %all-gather.2.cloned.1.call-update) | async-done | bytes 3276816 | tf_op jit(solution)/shard_map/all_gather | solution.py:125
  72.5 0.0 reduce-scatter.2.cloned.1.call-update
  72.5 1.9 %copy-done = bf16[2560,640]{1,0:T(8,128)(2,1)S(1)} copy-done((bf16[2560,640]{1,0:T(8,128)(2,1)S(1)}, bf16[2560,640]{1,0:T(8,128)(2,1)}, u32[]{:S(2)}) %copy-start) | copy-done | bytes 3276824
  74.4 5.0 %shard_map.59 = (bf16[2,2,384,640]{3,2,1,0:T(8,128)(2,1)S(1)}, bf16[2,2,384,640]{3,2,1,0:T(8,128)(2,1)S(1)}) custom-call(s32[1]{0:T(128)} %bitcast.t, bf16[384,640]{1,0:T(8,128)(2,1)S(1)} %copy-done.2, bf16[384,640]{1,0:T(8,128)(2,1)} %collective-permute-done.refs_9_.c_far, bf16[4,640,640]{2,1,0:T(8,128)(2,1)S(1)} %bitcast.27), custom_call_target="tpu_custom_call" | custom-call | flops 2516582400 | bytes 8388608 | tf_op jit(solution)/shard_map/pallas_call | solution.py:142
  79.4 0.3 collective-permute-start.9
  79.7 4.9 %shard_map.60 = (bf16[384,640]{1,0:T(8,128)(2,1)S(1)}, bf16[384,640]{1,0:T(8,128)(2,1)S(1)}) custom-call(s32[1]{0:T(128)} %bitcast.t, bf16[384,640]{1,0:T(8,128)(2,1)S(1)} %get-tuple-element.21.refs_0_, bf16[384,640]{1,0:T(8,128)(2,1)S(1)} %collective-permute-done.1.refs_1_, bf16[384,640]{1,0:T(8,128)(2,1)S(1)} %collective-permute-done.2.refs_2_, ...), custom_call_target="tpu_custom_call" | custom-call | flops 2516582400 | bytes 8388608 | tf_op jit(solution)/shard_map/pallas_call | solution.py:149
  84.6 0.9 collective-permute-start.13
  85.5 0.5 add_convert_fusion
  86.1 1.2 slice_bitcast_fusion.2
  87.2 1.2 collective-permute-start.10
  88.4 0.9 collective-permute-start.11
  89.2 2.1 %collective-permute-start.12 = (bf16[384,640]{1,0:T(8,128)(2,1)}, bf16[384,640]{1,0:T(8,128)(2,1)}, u32[]{:S(2)}, u32[]{:S(2)}) collective-permute-start(bf16[384,640]{1,0:T(8,128)(2,1)} %get-tuple-element.18), channel_id=1, source_target_pairs={{0,20},{1,21},{2,22},{3,23},{4,16},{5,17},{6,18},{7,19},{8,28},{9,... | collective-permute-start | bytes 1474568 | tf_op jit(solution)/shard_map/ppermute | solution.py:29
  91.3 7.5 %collective-permute-done.13 = bf16[384,640]{1,0:T(8,128)(2,1)} collective-permute-done((bf16[384,640]{1,0:T(8,128)(2,1)S(1)}, bf16[384,640]{1,0:T(8,128)(2,1)}, u32[]{:S(2)}, u32[]{:S(2)}) %collective-permute-start.13) | collective-permute-done | bytes 491552 | tf_op jit(solution)/shard_map/ppermute | solution.py:29
  98.8 1.9 %add_convert_fusion.1 = bf16[384,640]{1,0:T(8,128)(2,1)} fusion(bf16[384,640]{1,0:T(8,128)(2,1)} %collective-permute-done.13, bf16[384,640]{1,0:T(8,128)(2,1)S(1)} %get-tuple-element.12), kind=kLoop, calls=%fused_computation.4 | loop fusion | flops 983040 | bytes 1474560 | tf_op jit(solution)/shard_map/convert_element_type | solution.py:150
  100.7 20.3 %reduce-scatter.2.cloned.1.call-done = bf16[1,4,80,640]{3,2,1,0:T(8,128)(2,1)} async-done(((bf16[8,4,80,640]{3,2,1,0:T(8,128)(2,1)}), bf16[1,4,80,640]{3,2,1,0:T(8,128)(2,1)}) %reduce-scatter.2.cloned.1.call-update) | async-done | bytes 409616 | tf_op jit(solution)/shard_map/reduce_scatter | solution.py:138
  121.1 1.0 dynamic-slice_bitcast_fusion.2
  122.1 1.4 collective-permute-start.14
  123.5 1.9 %collective-permute-start.15 = (bf16[80,640]{1,0:T(8,128)(2,1)S(1)}, bf16[80,640]{1,0:T(8,128)(2,1)S(1)}, u32[]{:S(2)}, u32[]{:S(2)}) collective-permute-start(bf16[80,640]{1,0:T(8,128)(2,1)S(1)} %get-tuple-element.24), channel_id=1, source_target_pairs={{0,3},{1,0},{2,1},{3,2},{4,7},{5,4},{6,5},{7,6},{8,11},{9,8},{10,9... | collective-permute-start | bytes 307208 | tf_op jit(solution)/shard_map/ppermute | solution.py:29
  125.4 1.8 %collective-permute-start.16 = (bf16[80,640]{1,0:T(8,128)(2,1)S(1)}, bf16[80,640]{1,0:T(8,128)(2,1)S(1)}, u32[]{:S(2)}, u32[]{:S(2)}) collective-permute-start(bf16[80,640]{1,0:T(8,128)(2,1)S(1)} %get-tuple-element.23), channel_id=1, source_target_pairs={{0,2},{1,3},{2,0},{3,1},{4,6},{5,7},{6,4},{7,5},{8,10},{9,11},{10,... | collective-permute-start | bytes 307208 | tf_op jit(solution)/shard_map/ppermute | solution.py:29
  127.2 1.5 broadcast_select_fusion.1
  128.7 0.5 collective-permute-done.14
  129.1 2.4 %collective-permute-done.16 = bf16[80,640]{1,0:T(8,128)(2,1)S(1)} collective-permute-done((bf16[80,640]{1,0:T(8,128)(2,1)S(1)}, bf16[80,640]{1,0:T(8,128)(2,1)S(1)}, u32[]{:S(2)}, u32[]{:S(2)}) %collective-permute-start.16) | collective-permute-done | bytes 102432 | tf_op jit(solution)/shard_map/ppermute | solution.py:29
  131.6 1.0 fusion.3
  132.5 2.9 %collective-permute-start.17 = (bf16[80,640]{1,0:T(8,128)(2,1)S(1)}, bf16[80,640]{1,0:T(8,128)(2,1)S(1)}, u32[]{:S(2)}, u32[]{:S(2)}) collective-permute-start(bf16[80,640]{1,0:T(8,128)(2,1)S(1)} %fusion.3), channel_id=1, source_target_pairs={{0,0},{1,1},{2,2},{3,3},{4,32},{5,33},{6,34},{7,35},{8,8},{9,9},{1... | collective-permute-start | bytes 307208 | tf_op jit(solution)/shard_map/ppermute | solution.py:29
  135.5 1.0 pad_maximum_fusion
  136.5 3.5 %collective-permute-done.17 = bf16[80,640]{1,0:T(8,128)(2,1)S(1)} collective-permute-done((bf16[80,640]{1,0:T(8,128)(2,1)S(1)}, bf16[80,640]{1,0:T(8,128)(2,1)S(1)}, u32[]{:S(2)}, u32[]{:S(2)}) %collective-permute-start.17) | collective-permute-done | bytes 102432 | tf_op jit(solution)/shard_map/ppermute | solution.py:29
  140.0 0.7 convert_element_type.79
  (20 shorter events, 0.0 us)
Async XLA Ops:
  7.2 16.4 %copy-start.5 = (bf16[384,1280]{1,0:T(8,128)(2,1)S(1)}, bf16[384,1280]{1,0:T(8,128)(2,1)}, u32[]{:S(2)}) copy-start(bf16[384,1280]{1,0:T(8,128)(2,1)} %param.5) | copy-start | bytes 2949124
  7.2 65.3 %all-gather.2.cloned.1.call-start = ((), (), s32[]{:S(2)}) async-start(), calls=%async_computation.1 | async-start | bytes 3686400 | tf_op jit(solution)/shard_map/all_gather | solution.py:125
  8.4 19.5 %copy-start.2 = (bf16[384,640]{1,0:T(8,128)(2,1)S(1)}, bf16[384,640]{1,0:T(8,128)(2,1)}, u32[]{:S(2)}) copy-start(bf16[384,640]{1,0:T(8,128)(2,1)} %c_own.1) | copy-start | bytes 1474564
  8.4 13.2 %collective-permute-start.8 = (bf16[320,640]{1,0:T(8,128)(2,1)S(1)}, bf16[320,640]{1,0:T(8,128)(2,1)S(1)}, u32[]{:S(2)}, u32[]{:S(2)}) collective-permute-start(bf16[320,640]{1,0:T(8,128)(2,1)S(1)} %constant_dynamic-slice_fusion), channel_id=1, source_target_pairs={{0,32},{1,33},{2,34},{3,35},{8,40},{9,41},{10,42},{11,43},{16,48},... | collective-permute-start | bytes 1228808 | tf_op jit(solution)/shard_map/ppermute | solution.py:29
  23.5 97.6 %reduce-scatter.2.cloned.1.call-start = ((), (), s32[]{:S(2)}) async-start(), calls=%async_computation.2 | async-start | bytes 3686400 | tf_op jit(solution)/shard_map/reduce_scatter | solution.py:138
  23.6 15.8 %collective-permute-start.2 = (bf16[384,640]{1,0:T(8,128)(2,1)S(1)}, bf16[384,640]{1,0:T(8,128)(2,1)S(1)}, u32[]{:S(2)}, u32[]{:S(2)}) collective-permute-start(bf16[384,640]{1,0:T(8,128)(2,1)S(1)} %get-tuple-element.21.refs_0_), channel_id=1, source_target_pairs={{0,16},{1,17},{2,18},{3,19},{4,20},{5,21},{6,22},{7,23},{8,24},{9,... | collective-permute-start | bytes 1474568 | tf_op jit(solution)/shard_map/ppermute | solution.py:29
  25.1 22.3 %collective-permute-start.4 = (bf16[384,640]{1,0:T(8,128)(2,1)S(1)}, bf16[384,640]{1,0:T(8,128)(2,1)S(1)}, u32[]{:S(2)}, u32[]{:S(2)}) collective-permute-start(bf16[384,640]{1,0:T(8,128)(2,1)S(1)} %get-tuple-element.20), channel_id=1, source_target_pairs={{0,4},{1,5},{2,6},{3,7},{4,0},{5,1},{6,2},{7,3},{8,12},{9,13},{10,... | collective-permute-start | bytes 1474568 | tf_op jit(solution)/shard_map/ppermute | solution.py:29
  25.1 22.7 %collective-permute-start.6 = (bf16[384,640]{1,0:T(8,128)(2,1)S(1)}, bf16[384,640]{1,0:T(8,128)(2,1)S(1)}, u32[]{:S(2)}, u32[]{:S(2)}) collective-permute-start(bf16[384,640]{1,0:T(8,128)(2,1)S(1)} %get-tuple-element.20), channel_id=1, source_target_pairs={{0,20},{1,21},{2,22},{3,23},{4,16},{5,17},{6,18},{7,19},{8,28},{9,... | collective-permute-start | bytes 1474568 | tf_op jit(solution)/shard_map/ppermute | solution.py:29
  27.8 20.2 %collective-permute-start.1 = (bf16[384,640]{1,0:T(8,128)(2,1)S(1)}, bf16[384,640]{1,0:T(8,128)(2,1)S(1)}, u32[]{:S(2)}, u32[]{:S(2)}) collective-permute-start(bf16[384,640]{1,0:T(8,128)(2,1)S(1)} %get-tuple-element.21.refs_0_), channel_id=1, source_target_pairs={{0,8},{1,9},{2,10},{3,11},{4,12},{5,13},{6,14},{7,15},{8,0},{9,1},... | collective-permute-start | bytes 1474568 | tf_op jit(solution)/shard_map/ppermute | solution.py:29
  27.8 28.0 %collective-permute-start = (bf16[384,640]{1,0:T(8,128)(2,1)S(1)}, bf16[384,640]{1,0:T(8,128)(2,1)}, u32[]{:S(2)}, u32[]{:S(2)}) collective-permute-start(bf16[384,640]{1,0:T(8,128)(2,1)S(1)} %copy-done.2), channel_id=1, source_target_pairs={{0,4},{1,5},{2,6},{3,7},{4,0},{5,1},{6,2},{7,3},{8,12},{9,13},{10,... | collective-permute-start | bytes 1474568 | tf_op jit(solution)/shard_map/ppermute | solution.py:29
  39.4 16.4 %collective-permute-start.3 = (bf16[384,640]{1,0:T(8,128)(2,1)S(1)}, bf16[384,640]{1,0:T(8,128)(2,1)S(1)}, u32[]{:S(2)}, u32[]{:S(2)}) collective-permute-start(bf16[384,640]{1,0:T(8,128)(2,1)S(1)} %collective-permute-done.2.refs_2_), channel_id=1, source_target_pairs={{0,8},{1,9},{2,10},{3,11},{4,12},{5,13},{6,14},{7,15},{8,0},{9,1},... | collective-permute-start | bytes 1474568 | tf_op jit(solution)/shard_map/ppermute | solution.py:29
  47.4 8.5 %collective-permute-start.5 = (bf16[384,640]{1,0:T(8,128)(2,1)S(1)}, bf16[384,640]{1,0:T(8,128)(2,1)}, u32[]{:S(2)}, u32[]{:S(2)}) collective-permute-start(bf16[384,640]{1,0:T(8,128)(2,1)S(1)} %collective-permute-done.4.refs_4_), channel_id=1, source_target_pairs={{0,8},{1,9},{2,10},{3,11},{4,12},{5,13},{6,14},{7,15},{8,0},{9,1},... | collective-permute-start | bytes 1474568 | tf_op jit(solution)/shard_map/ppermute | solution.py:29
  47.9 8.0 %collective-permute-start.7 = (bf16[384,640]{1,0:T(8,128)(2,1)S(1)}, bf16[384,640]{1,0:T(8,128)(2,1)}, u32[]{:S(2)}, u32[]{:S(2)}) collective-permute-start(bf16[384,640]{1,0:T(8,128)(2,1)S(1)} %collective-permute-done.6.refs_6_), channel_id=1, source_target_pairs={{0,8},{1,9},{2,10},{3,11},{4,12},{5,13},{6,14},{7,15},{8,0},{9,1},... | collective-permute-start | bytes 1474568 | tf_op jit(solution)/shard_map/ppermute | solution.py:29
  55.9 7.2 %copy-start.3 = (bf16[384,640]{1,0:T(8,128)(2,1)}, bf16[384,640]{1,0:T(8,128)(2,1)S(1)}, u32[]{:S(2)}) copy-start(bf16[384,640]{1,0:T(8,128)(2,1)S(1)} %collective-permute-done.3.refs_3_) | copy-start | bytes 1474564
  72.5 1.9 %copy-start = (bf16[2560,640]{1,0:T(8,128)(2,1)S(1)}, bf16[2560,640]{1,0:T(8,128)(2,1)}, u32[]{:S(2)}) copy-start(bf16[2560,640]{1,0:T(8,128)(2,1)} %all-gather.2.cloned.1.call-done) | copy-start | bytes 9830404
  74.4 5.3 %copy-start.1 = (bf16[2560,640]{1,0:T(8,128)(2,1)S(1)}, bf16[2560,640]{1,0:T(8,128)(2,1)}, u32[]{:S(2)}) copy-start(bf16[2560,640]{1,0:T(8,128)(2,1)} %all-gather.2.cloned.1.call-done) | copy-start | bytes 9830404
  74.4 5.3 %copy-start.4 = (bf16[384,640]{1,0:T(8,128)(2,1)S(1)}, bf16[384,640]{1,0:T(8,128)(2,1)}, u32[]{:S(2)}) copy-start(bf16[384,640]{1,0:T(8,128)(2,1)} %copy-done.3) | copy-start | bytes 1474564
  79.4 6.1 %collective-permute-start.9 = (bf16[2,2,384,640]{3,2,1,0:T(8,128)(2,1)S(1)}, bf16[2,2,384,640]{3,2,1,0:T(8,128)(2,1)S(1)}, u32[]{:S(2)}, u32[]{:S(2)}) collective-permute-start(bf16[2,2,384,640]{3,2,1,0:T(8,128)(2,1)S(1)} %get-tuple-element.11), channel_id=1, source_target_pairs={{0,8},{1,9},{2,10},{3,11},{4,12},{5,13},{6,14},{7,15},{8,0},{9,1},... | collective-permute-start | bytes 5898248 | tf_op jit(solution)/shard_map/ppermute | solution.py:29
  84.6 14.2 %collective-permute-start.13 = (bf16[384,640]{1,0:T(8,128)(2,1)S(1)}, bf16[384,640]{1,0:T(8,128)(2,1)}, u32[]{:S(2)}, u32[]{:S(2)}) collective-permute-start(bf16[384,640]{1,0:T(8,128)(2,1)S(1)} %get-tuple-element.13), channel_id=1, source_target_pairs={{0,4},{1,5},{2,6},{3,7},{4,0},{5,1},{6,2},{7,3},{8,12},{9,13},{10,... | collective-permute-start | bytes 1474568 | tf_op jit(solution)/shard_map/ppermute | solution.py:29
  87.2 38.2 %collective-permute-start.10 = (bf16[384,640]{1,0:T(8,128)(2,1)}, bf16[384,640]{1,0:T(8,128)(2,1)S(1)}, u32[]{:S(2)}, u32[]{:S(2)}) collective-permute-start(bf16[384,640]{1,0:T(8,128)(2,1)} %get-tuple-element.17), channel_id=1, source_target_pairs={{0,16},{1,17},{2,18},{3,19},{4,20},{5,21},{6,22},{7,23},{8,24},{9,... | collective-permute-start | bytes 1474568 | tf_op jit(solution)/shard_map/ppermute | solution.py:29
  88.4 38.8 %collective-permute-start.11 = (bf16[384,640]{1,0:T(8,128)(2,1)}, bf16[384,640]{1,0:T(8,128)(2,1)}, u32[]{:S(2)}, u32[]{:S(2)}) collective-permute-start(bf16[384,640]{1,0:T(8,128)(2,1)} %get-tuple-element.19), channel_id=1, source_target_pairs={{0,4},{1,5},{2,6},{3,7},{4,0},{5,1},{6,2},{7,3},{8,12},{9,13},{10,... | collective-permute-start | bytes 1474568 | tf_op jit(solution)/shard_map/ppermute | solution.py:29
  89.2 37.9 %collective-permute-start.12 = (bf16[384,640]{1,0:T(8,128)(2,1)}, bf16[384,640]{1,0:T(8,128)(2,1)}, u32[]{:S(2)}, u32[]{:S(2)}) collective-permute-start(bf16[384,640]{1,0:T(8,128)(2,1)} %get-tuple-element.18), channel_id=1, source_target_pairs={{0,20},{1,21},{2,22},{3,23},{4,16},{5,17},{6,18},{7,19},{8,28},{9,... | collective-permute-start | bytes 1474568 | tf_op jit(solution)/shard_map/ppermute | solution.py:29
  122.1 7.0 %collective-permute-start.14 = (bf16[80,640]{1,0:T(8,128)(2,1)S(1)}, bf16[80,640]{1,0:T(8,128)(2,1)S(1)}, u32[]{:S(2)}, u32[]{:S(2)}) collective-permute-start(bf16[80,640]{1,0:T(8,128)(2,1)S(1)} %get-tuple-element.22), channel_id=1, source_target_pairs={{0,1},{1,2},{2,3},{3,0},{4,5},{5,6},{6,7},{7,4},{8,9},{9,10},{10,1... | collective-permute-start | bytes 307208 | tf_op jit(solution)/shard_map/ppermute | solution.py:29
  123.5 5.7 %collective-permute-start.15 = (bf16[80,640]{1,0:T(8,128)(2,1)S(1)}, bf16[80,640]{1,0:T(8,128)(2,1)S(1)}, u32[]{:S(2)}, u32[]{:S(2)}) collective-permute-start(bf16[80,640]{1,0:T(8,128)(2,1)S(1)} %get-tuple-element.24), channel_id=1, source_target_pairs={{0,3},{1,0},{2,1},{3,2},{4,7},{5,4},{6,5},{7,6},{8,11},{9,8},{10,9... | collective-permute-start | bytes 307208 | tf_op jit(solution)/shard_map/ppermute | solution.py:29
  125.4 6.2 %collective-permute-start.16 = (bf16[80,640]{1,0:T(8,128)(2,1)S(1)}, bf16[80,640]{1,0:T(8,128)(2,1)S(1)}, u32[]{:S(2)}, u32[]{:S(2)}) collective-permute-start(bf16[80,640]{1,0:T(8,128)(2,1)S(1)} %get-tuple-element.23), channel_id=1, source_target_pairs={{0,2},{1,3},{2,0},{3,1},{4,6},{5,7},{6,4},{7,5},{8,10},{9,11},{10,... | collective-permute-start | bytes 307208 | tf_op jit(solution)/shard_map/ppermute | solution.py:29
  132.5 7.5 %collective-permute-start.17 = (bf16[80,640]{1,0:T(8,128)(2,1)S(1)}, bf16[80,640]{1,0:T(8,128)(2,1)S(1)}, u32[]{:S(2)}, u32[]{:S(2)}) collective-permute-start(bf16[80,640]{1,0:T(8,128)(2,1)S(1)} %fusion.3), channel_id=1, source_target_pairs={{0,0},{1,1},{2,2},{3,3},{4,32},{5,33},{6,34},{7,35},{8,8},{9,9},{1... | collective-permute-start | bytes 307208 | tf_op jit(solution)/shard_map/ppermute | solution.py:29
Sparse Core Ops, SparseCore 0:
  23.6 48.8 all-gather.1
  75.0 45.9 reduce-scatter.1

commit v3 on v2

v3 whole, which is shorter than its diff:
```python
import jax
import jax.numpy as jnp
from jax import lax
from jax.experimental import pallas as pl
from jax.experimental.pallas import tpu as pltpu
from jax.sharding import PartitionSpec as P

BF, F32 = jnp.bfloat16, jnp.float32
ALL = ("blk", "tp", "rep")
WORK = 2 * 768 * 2560 * 640


def number(z, a, k, l, y):
    return (z * 4 + a * 2 + k) * 8 + l * 4 + y


def places():
    for z in range(8):
        for a in range(2):
            for k in range(2):
                for l in range(2):
                    for y in range(4):
                        yield z, a, k, l, y


def move(value, target):
    return lax.ppermute(value, ALL, [(number(*p), number(*target(*p))) for p in places()])


def swap_core(v):
    return move(v, lambda z, a, k, l, y: (z, a, 1 - k, l, y))


def swap_lo(v):
    return move(v, lambda z, a, k, l, y: (z, a, k, 1 - l, y))


def swap_hi(v):
    return move(v, lambda z, a, k, l, y: (z, 1 - a, k, l, y))


def swap_both(v):
    return move(v, lambda z, a, k, l, y: (z, 1 - a, k, 1 - l, y))


def to_y(v, d):
    return move(v, lambda z, a, k, l, y: (z, a, k, l, (y + d) % 4))


def dot(a, b, ca, cb):
    return lax.dot_general(a, b, (((ca,), (cb,)), ((), ())), preferred_element_type=F32)


def add(*terms):
    total = terms[0].astype(F32)
    for term in terms[1:]:
        total = total + term.astype(F32)
    return total


def pick(v, i, axis):
    return lax.dynamic_index_in_dim(v, i, axis, keepdims=False)


def over_y(v, y):
    return add(pick(v, y, 0), *(to_y(pick(v, (y + d) % 4, 0), d) for d in (1, 3, 2)))


def call(kernel, outs, flops, n_in):
    whole = pl.BlockSpec(memory_space=pltpu.VMEM)
    return pl.pallas_call(
        kernel,
        out_shape=[jax.ShapeDtypeStruct(s, BF) for s in outs],
        in_specs=[pl.BlockSpec(memory_space=pltpu.SMEM)] + [whole] * n_in,
        out_specs=[whole] * len(outs),
        compiler_params=pltpu.CompilerParams(vmem_limit_bytes=40 << 20),
        cost_estimate=pl.CostEstimate(flops=flops, bytes_accessed=8 << 20, transcendentals=0),
    )


def split_kernel(at, g, mine, theirs):
    for f in range(2):

        @pl.when(at[1] == f)
        def _():
            for i in range(2):
                mine[:, i * 320 : i * 320 + 320] = g[:, i * 640 + f * 320 : i * 640 + f * 320 + 320]
                theirs[:, i * 320 : i * 320 + 320] = g[:, i * 640 + 320 - f * 320 : i * 640 + 640 - f * 320]


def join_kernel(at, keep, hi, lo, both, out):
    first = (keep[0, 1].astype(F32) + hi[...].astype(F32)).astype(BF)
    second = (lo[...].astype(F32) + both[...].astype(F32)).astype(BF)
    for f in range(2):

        @pl.when(at[1] == f)
        def _():
            for i in range(2):
                out[:, i * 640 + f * 320 : i * 640 + f * 320 + 320] = first[:, i * 320 : i * 320 + 320]
                out[:, i * 640 + 320 - f * 320 : i * 640 + 640 - f * 320] = second[:, i * 320 : i * 320 + 320]


def gw_kernel(at, *refs):
    g_own, g_far, c_own, c_far, out = refs[:4], refs[4:8], refs[8], refs[9], refs[10]
    for q in range(4):
        out[at[0] ^ q] = (dot(g_own[q][...], c_own[...], 0, 0) + dot(g_far[q][...], c_far[...], 0, 0)).astype(BF)


def proj_kernel(at, c_own, c_far, w, *outs):
    for q in (1, 3, 0, 2):
        for s, c in enumerate((c_far, c_own)):
            outs[q % 2][q // 2, s] = dot(c[...], w[at[0] ^ q], 1, 1).astype(BF)


def gc_kernel(at, *refs):
    w, far, own = refs[8:]
    for g, out in ((refs[4:8], far), (refs[:4], own)):
        total = dot(g[0][...], w[at[0]], 1, 0)
        for q in range(1, 4):
            total += dot(g[q][...], w[at[0] ^ q], 1, 0)
        out[...] = total.astype(BF)


def body(context, out_weight, grad_out):
    t = lax.axis_index("tp")
    r = lax.axis_index("rep")
    f, y = r // 4, r % 4
    at = jnp.stack([t, f]).astype(jnp.int32)

    half = lax.dynamic_slice_in_dim(out_weight, f * 320, 320, 0)
    weight = lax.all_gather(half, "blk", axis=0, tiled=True)

    c_far = swap_lo(context)
    g_mine, g_theirs = call(split_kernel, [(384, 640)] * 2, 0, 1)(at, grad_out)
    near = swap_lo(g_theirs)
    cross = swap_both(g_theirs)
    hi = swap_hi(g_mine)
    own = [g_mine, swap_core(g_mine), hi, swap_core(hi)]
    far = [near, swap_core(near), cross, swap_core(cross)]

    gw = call(gw_kernel, [(4, 640, 640)], WORK, 10)(at, *own, *far, context, c_far)[0]
    gw, weight = lax.optimization_barrier((gw, weight))
    gw = lax.psum_scatter(gw.reshape(8, 4, 80, 640), "blk", scatter_dimension=0, tiled=True)
    grad_weight = over_y(gw[0], y)

    w = weight.reshape(4, 640, 640)
    keep, give = call(proj_kernel, [(2, 2, 384, 640)] * 2, WORK, 3)(at, context, c_far, w)
    keep = add(keep, swap_core(give)).astype(BF)
    parts = keep, swap_hi(keep[1, 1]), swap_lo(keep[0, 0]), swap_both(keep[1, 0])
    projected = call(join_kernel, [(384, 1280)], 0, 4)(at, *parts)[0]

    gc_far, gc_own = call(gc_kernel, [(384, 640)] * 2, WORK, 9)(at, *own, *far, w)
    grad_context = add(gc_own, swap_lo(gc_far)).astype(BF)
    return projected, grad_context, grad_weight


def solution(mesh):
    spec = P(("blk", "rep"), "tp")
    return jax.shard_map(
        body,
        mesh=mesh,
        in_specs=(spec, P("blk", "tp"), spec),
        out_specs=(spec, spec, spec),
        check_vma=False,
    )
```

time: 148 us -> 127 us (0.86)
  waiting for transfers between devices: 83.1 us -> 63 us
  local copies, waits for them, and re-layouts: 5.33 us -> 12.8 us
  other arithmetic: 8.43 us -> 4.12 us
  starting transfers between devices: 19.4 us -> 16 us
    ppermute x18 -> x16, waiting for transfers between devices: 53.3 us -> 27.7 us  [move(): lax.ppermute(value, ALL, [(number(*p), number(*target(*p))) for p in plac...]
    reduce_scatter x1, waiting for transfers between devices: 20.3 us -> 31 us  [body(): lax.psum_scatter(gw.reshape(8, 4, 80, 640), 'blk', scatter_dimension=0, t...]
    unnamed x12 -> x30, local copies, waits for them, and re-layouts: 1.94 us -> 9.85 us
    all_gather x1, waiting for transfers between devices: 9.47 us -> 4.25 us  [body(): weight = lax.all_gather(half, 'blk', axis=0, tiled=True)]
    pallas_call x0 -> x2, Pallas kernels: none -> 3.65 us  [the longest x1 2.83 us: body(): projected = call(join_kernel, [(384, 1280)], 0, 4)(at, *parts)[0]]
    ppermute x18 -> x16, starting transfers between devices: 19.4 us -> 15.9 us  [move(): lax.ppermute(value, ALL, [(number(*p), number(*target(*p))) for p in plac...]
    select_n x2 -> x0, other arithmetic: 3.33 us -> none  [the longest x1 1.85 us: body(): part = jnp.where(z % 2 == f, mine, move(part, to_pair))]
    pallas_call x1, Pallas kernels: 7.14 us -> 4.5 us  [body(): call(gw_kernel, [(4, 640, 640)], WORK, 10)(at, *own, *far, context, c_far)]
  transfers between devices with their start and end apart: 20 -> 18, of which waited for: 11 -> 5; matrix products, arithmetic and copies ran while one was open for 5% -> 4% of each run, Pallas kernels for 12% -> 13%
where the time goes in v3:
time: 127 us
  waiting for transfers between devices  63 us (50%)
  Pallas kernels  16.7 us (13%)
  starting transfers between devices  16 us (13%)
  between operations  14.2 us (11%)
  local copies, waits for them, and re-layouts  12.8 us (10%)
  other arithmetic  4.12 us (3%)
    reduce_scatter x1, waiting for transfers between devices, body(): lax.psum_scatter(gw.reshape(8, 4, 80, 640), 'blk', scatter_dimension=0, t...  31 us
    ppermute x16, waiting for transfers between devices, move(): lax.ppermute(value, ALL, [(number(*p), number(*target(*p))) for p in plac...  27.7 us
    ppermute x16, starting transfers between devices, move(): lax.ppermute(value, ALL, [(number(*p), number(*target(*p))) for p in plac...  15.9 us
    unnamed x30, local copies, waits for them, and re-layouts  9.85 us
    pallas_call x1, Pallas kernels, body(): call(gw_kernel, [(4, 640, 640)], WORK, 10)(at, *own, *far, context, c_far)  4.5 us
    pallas_call x1, Pallas kernels, body(): call(proj_kernel, [(2, 2, 384, 640)] * 2, WORK, 3)(at, context, c_far, w)  4.35 us
    all_gather x1, waiting for transfers between devices, body(): weight = lax.all_gather(half, 'blk', axis=0, tiled=True)  4.25 us
    pallas_call x1, Pallas kernels, body(): call(gc_kernel, [(384, 640)] * 2, WORK, 9)(at, *own, *far, w)  4.2 us
  transfers between devices with their start and end apart: 18, of which 5 were waited for; matrix products, arithmetic and copies ran while one was open for 4% of the time, Pallas kernels for 13%

profile of v3, /device:TPU:6, one launch (start us, length us, event | category | flops | bytes accessed | tf_op | source)
XLA Modules:
  0.0 126.9 jit_solution(10803725274202232473)
XLA Ops:
  7.2 0.0 copy-start
  7.2 0.0 all-gather.2.cloned.1.call-start
  7.3 1.1 copy-done
  8.3 0.8 constant_dynamic-slice_fusion
  9.1 0.0 all-gather.2.cloned.1.call-update
  9.1 0.0 reduce-scatter.2.cloned.1.call-start
  9.2 0.1 pad_add_fusion.at
  9.3 1.2 copy-done.2
  10.5 0.8 shard_map.58
  11.3 1.5 %collective-permute-start.2 = (bf16[384,640]{1,0:T(8,128)(2,1)S(1)}, bf16[384,640]{1,0:T(8,128)(2,1)S(1)}, u32[]{:S(2)}, u32[]{:S(2)}) collective-permute-start(bf16[384,640]{1,0:T(8,128)(2,1)S(1)} %get-tuple-element.11.refs_0_), channel_id=1, source_target_pairs={{0,16},{1,17},{2,18},{3,19},{4,20},{5,21},{6,22},{7,23},{8,24},{9,... | collective-permute-start | bytes 1474568 | tf_op jit(solution)/shard_map/ppermute | solution.py:27
  12.8 1.7 %collective-permute-start.4 = (bf16[384,640]{1,0:T(8,128)(2,1)S(1)}, bf16[384,640]{1,0:T(8,128)(2,1)S(1)}, u32[]{:S(2)}, u32[]{:S(2)}) collective-permute-start(bf16[384,640]{1,0:T(8,128)(2,1)S(1)} %get-tuple-element.12), channel_id=1, source_target_pairs={{0,4},{1,5},{2,6},{3,7},{4,0},{5,1},{6,2},{7,3},{8,12},{9,13},{10,... | collective-permute-start | bytes 1474568 | tf_op jit(solution)/shard_map/ppermute | solution.py:27
  14.5 1.0 collective-permute-start.6
  15.5 0.0 collective-permute-start.1
  15.5 0.8 collective-permute-start
  16.3 10.7 %collective-permute-done.2.refs_2_ = bf16[384,640]{1,0:T(8,128)(2,1)S(1)} collective-permute-done((bf16[384,640]{1,0:T(8,128)(2,1)S(1)}, bf16[384,640]{1,0:T(8,128)(2,1)S(1)}, u32[]{:S(2)}, u32[]{:S(2)}) %collective-permute-start.2) | collective-permute-done | bytes 491552 | tf_op jit(solution)/shard_map/ppermute | solution.py:27
  27.0 0.0 collective-permute-start.3
  27.0 10.1 %collective-permute-done.4.refs_4_ = bf16[384,640]{1,0:T(8,128)(2,1)S(1)} collective-permute-done((bf16[384,640]{1,0:T(8,128)(2,1)S(1)}, bf16[384,640]{1,0:T(8,128)(2,1)S(1)}, u32[]{:S(2)}, u32[]{:S(2)}) %collective-permute-start.4) | collective-permute-done | bytes 491552 | tf_op jit(solution)/shard_map/ppermute | solution.py:27
  37.2 0.0 collective-permute-done.6.refs_6_
  37.2 0.5 collective-permute-start.7
  37.7 0.0 collective-permute-done.1.refs_1_
  37.7 6.9 %collective-permute-done.refs_9_.c_far = bf16[384,640]{1,0:T(8,128)(2,1)S(1)} collective-permute-done((bf16[384,640]{1,0:T(8,128)(2,1)S(1)}, bf16[384,640]{1,0:T(8,128)(2,1)S(1)}, u32[]{:S(2)}, u32[]{:S(2)}) %collective-permute-start) | collective-permute-done | bytes 491552 | tf_op jit(solution)/shard_map/ppermute | solution.py:27
  44.6 4.5 %shard_map.59 = bf16[4,640,640]{2,1,0:T(8,128)(2,1)S(1)} custom-call(s32[2]{0:T(128)S(1)} %pad_add_fusion.at, bf16[384,640]{1,0:T(8,128)(2,1)S(1)} %get-tuple-element.11.refs_0_, bf16[384,640]{1,0:T(8,128)(2,1)S(1)} %collective-permute-done.1.refs_1_, bf16[384,640]{1,0:T(8,128)(2,1)S(1)} %collective-permute-done.2.refs_2_, ...), custom_call_target="tpu_custom_call" | custom-call | flops 2516582400 | bytes 8388608 | tf_op jit(solution)/shard_map/pallas_call | solution.py:141
  49.1 1.7 %copy-done.1 = bf16[4,640,640]{2,1,0:T(8,128)(2,1)} copy-done((bf16[4,640,640]{2,1,0:T(8,128)(2,1)}, bf16[4,640,640]{2,1,0:T(8,128)(2,1)S(1)}, u32[]{:S(2)}) %copy-start.1) | copy-done | bytes 3276824
  50.8 0.8 copy-done.5
  51.5 0.8 copy-done.7
  52.3 0.8 copy-done.9
  53.1 0.8 copy-done.11
  53.9 0.8 copy-done.13
  54.7 4.2 %all-gather.2.cloned.1.call-done = bf16[2560,640]{1,0:T(8,128)(2,1)} async-done(((bf16[320,640]{1,0:T(8,128)(2,1)}), bf16[2560,640]{1,0:T(8,128)(2,1)}) %all-gather.2.cloned.1.call-update) | async-done | bytes 3276816 | tf_op jit(solution)/shard_map/all_gather | solution.py:131
  59.0 0.0 reduce-scatter.2.cloned.1.call-update
  59.0 1.9 %copy-done.3 = bf16[2560,640]{1,0:T(8,128)(2,1)S(1)} copy-done((bf16[2560,640]{1,0:T(8,128)(2,1)S(1)}, bf16[2560,640]{1,0:T(8,128)(2,1)}, u32[]{:S(2)}) %copy-start.3) | copy-done | bytes 3276824
  60.9 4.4 %shard_map.60 = (bf16[2,2,384,640]{3,2,1,0:T(8,128)(2,1)S(1)}, bf16[2,2,384,640]{3,2,1,0:T(8,128)(2,1)S(1)}) custom-call(s32[2]{0:T(128)S(1)} %pad_add_fusion.at, bf16[384,640]{1,0:T(8,128)(2,1)S(1)} %copy-done.4, bf16[384,640]{1,0:T(8,128)(2,1)S(1)} %collective-permute-done.refs_9_.c_far, bf16[4,640,640]{2,1,0:T(8,128)(2,1)S(1)} %bitcast.20), custom_call_target="tpu_custom_call" | custom-call | flops 2516582400 | bytes 8388608 | tf_op jit(solution)/shard_map/pallas_call | solution.py:147
  65.3 0.3 collective-permute-start.8
  65.6 4.2 %shard_map.62 = (bf16[384,640]{1,0:T(8,128)(2,1)}, bf16[384,640]{1,0:T(8,128)(2,1)S(1)}) custom-call(s32[2]{0:T(128)S(1)} %pad_add_fusion.at, bf16[384,640]{1,0:T(8,128)(2,1)S(1)} %get-tuple-element.11.refs_0_, bf16[384,640]{1,0:T(8,128)(2,1)S(1)} %copy-done.8, bf16[384,640]{1,0:T(8,128)(2,1)S(1)} %collective-permute-done.2.refs_2_, ...), custom_call_target="tpu_custom_call" | custom-call | flops 2516582400 | bytes 8388608 | tf_op jit(solution)/shard_map/pallas_call | solution.py:152
  69.8 0.9 collective-permute-start.12
  70.8 0.5 add_convert_fusion.keep
  71.3 1.1 slice_bitcast_fusion
  72.4 1.2 collective-permute-start.10
  73.6 0.5 collective-permute-start.11
  74.1 2.4 %collective-permute-start.9 = (bf16[384,640]{1,0:T(8,128)(2,1)}, bf16[384,640]{1,0:T(8,128)(2,1)}, u32[]{:S(2)}, u32[]{:S(2)}) collective-permute-start(bf16[384,640]{1,0:T(8,128)(2,1)} %get-tuple-element.21), channel_id=1, source_target_pairs={{0,16},{1,17},{2,18},{3,19},{4,20},{5,21},{6,22},{7,23},{8,24},{9,... | collective-permute-start | bytes 1474568 | tf_op jit(solution)/shard_map/ppermute | solution.py:27
  76.5 31.0 %reduce-scatter.2.cloned.1.call-done = bf16[1,4,80,640]{3,2,1,0:T(8,128)(2,1)} async-done(((bf16[8,4,80,640]{3,2,1,0:T(8,128)(2,1)}), bf16[1,4,80,640]{3,2,1,0:T(8,128)(2,1)}) %reduce-scatter.2.cloned.1.call-update) | async-done | bytes 409616 | tf_op jit(solution)/shard_map/reduce_scatter | solution.py:143
  107.5 1.0 dynamic-slice_bitcast_fusion.2
  108.5 1.6 %collective-permute-start.13 = (bf16[80,640]{1,0:T(8,128)(2,1)S(1)}, bf16[80,640]{1,0:T(8,128)(2,1)S(1)}, u32[]{:S(2)}, u32[]{:S(2)}) collective-permute-start(bf16[80,640]{1,0:T(8,128)(2,1)S(1)} %get-tuple-element.22), channel_id=1, source_target_pairs={{0,1},{1,2},{2,3},{3,0},{4,5},{5,6},{6,7},{7,4},{8,9},{9,10},{10,1... | collective-permute-start | bytes 307208 | tf_op jit(solution)/shard_map/ppermute | solution.py:27
  110.1 1.8 %collective-permute-start.14 = (bf16[80,640]{1,0:T(8,128)(2,1)S(1)}, bf16[80,640]{1,0:T(8,128)(2,1)S(1)}, u32[]{:S(2)}, u32[]{:S(2)}) collective-permute-start(bf16[80,640]{1,0:T(8,128)(2,1)S(1)} %get-tuple-element.24), channel_id=1, source_target_pairs={{0,3},{1,0},{2,1},{3,2},{4,7},{5,4},{6,5},{7,6},{8,11},{9,8},{10,9... | collective-permute-start | bytes 307208 | tf_op jit(solution)/shard_map/ppermute | solution.py:27
  111.8 1.8 %collective-permute-start.15 = (bf16[80,640]{1,0:T(8,128)(2,1)S(1)}, bf16[80,640]{1,0:T(8,128)(2,1)S(1)}, u32[]{:S(2)}, u32[]{:S(2)}) collective-permute-start(bf16[80,640]{1,0:T(8,128)(2,1)S(1)} %get-tuple-element.23), channel_id=1, source_target_pairs={{0,2},{1,3},{2,0},{3,1},{4,6},{5,7},{6,4},{7,5},{8,10},{9,11},{10,... | collective-permute-start | bytes 307208 | tf_op jit(solution)/shard_map/ppermute | solution.py:27
  113.6 1.9 %add_convert_fusion.1 = bf16[384,640]{1,0:T(8,128)(2,1)} fusion(bf16[384,640]{1,0:T(8,128)(2,1)} %collective-permute-done.12, bf16[384,640]{1,0:T(8,128)(2,1)S(1)} %get-tuple-element.16), kind=kLoop, calls=%fused_computation.1 | loop fusion | flops 983040 | bytes 1474560 | tf_op jit(solution)/shard_map/convert_element_type | solution.py:153
  115.6 2.8 %shard_map.61 = bf16[384,1280]{1,0:T(8,128)(2,1)} custom-call(s32[2]{0:T(128)S(1)} %pad_add_fusion.at, bf16[2,2,384,640]{3,2,1,0:T(8,128)(2,1)S(1)} %add_convert_fusion.keep, bf16[384,640]{1,0:T(8,128)(2,1)} %collective-permute-done.9.hi, bf16[384,640]{1,0:T(8,128)(2,1)} %collective-permute-done.10.lo, bf16[384,640]{1,0:T(8,128)(2,1)} %collective-permute-done.11.both), custom_call_target="tpu_custom_call" | custom-call | bytes 8388608 | tf_op jit(solution)/shard_map/pallas_call | solution.py:150
  118.4 1.6 %fusion.1 = f32[80,640]{1,0:T(8,128)} fusion(bf16[80,640]{1,0:T(8,128)(2,1)S(1)} %collective-permute-done.15, bf16[80,640]{1,0:T(8,128)(2,1)S(1)} %collective-permute-done.14, bf16[80,640]{1,0:T(8,128)(2,1)S(1)} %collective-permute-done.13, bf16[1,4,80,640]{3,2,1,0:T(8,128)(2,1)} %reduce-scatter.2.cloned.1.call-done, s32[]{:T(128)S(6)} %select_n.42), kind=kLoop, calls=%fused_computation.7 | loop fusion | flops 358400 | bytes 614404 | tf_op jit(solution)/shard_map/add | solution.py:57
  (32 shorter events, 0.1 us)
Async XLA Ops:
  7.2 1.2 copy-start
  7.2 8.3 %copy-start.4 = (bf16[384,640]{1,0:T(8,128)(2,1)S(1)}, bf16[384,640]{1,0:T(8,128)(2,1)}, u32[]{:S(2)}) copy-start(bf16[384,640]{1,0:T(8,128)(2,1)} %c_own.1) | copy-start | bytes 1474564
  7.2 51.8 %all-gather.2.cloned.1.call-start = ((), (), s32[]{:S(2)}) async-start(), calls=%async_computation.1 | async-start | bytes 3686400 | tf_op jit(solution)/shard_map/all_gather | solution.py:131
  9.1 98.3 %reduce-scatter.2.cloned.1.call-start = ((), (), s32[]{:S(2)}) async-start(), calls=%async_computation.2 | async-start | bytes 3686400 | tf_op jit(solution)/shard_map/reduce_scatter | solution.py:143
  9.3 1.2 copy-start.2
  11.3 15.7 %collective-permute-start.2 = (bf16[384,640]{1,0:T(8,128)(2,1)S(1)}, bf16[384,640]{1,0:T(8,128)(2,1)S(1)}, u32[]{:S(2)}, u32[]{:S(2)}) collective-permute-start(bf16[384,640]{1,0:T(8,128)(2,1)S(1)} %get-tuple-element.11.refs_0_), channel_id=1, source_target_pairs={{0,16},{1,17},{2,18},{3,19},{4,20},{5,21},{6,22},{7,23},{8,24},{9,... | collective-permute-start | bytes 1474568 | tf_op jit(solution)/shard_map/ppermute | solution.py:27
  12.8 24.4 %collective-permute-start.4 = (bf16[384,640]{1,0:T(8,128)(2,1)S(1)}, bf16[384,640]{1,0:T(8,128)(2,1)S(1)}, u32[]{:S(2)}, u32[]{:S(2)}) collective-permute-start(bf16[384,640]{1,0:T(8,128)(2,1)S(1)} %get-tuple-element.12), channel_id=1, source_target_pairs={{0,4},{1,5},{2,6},{3,7},{4,0},{5,1},{6,2},{7,3},{8,12},{9,13},{10,... | collective-permute-start | bytes 1474568 | tf_op jit(solution)/shard_map/ppermute | solution.py:27
  14.5 22.7 %collective-permute-start.6 = (bf16[384,640]{1,0:T(8,128)(2,1)S(1)}, bf16[384,640]{1,0:T(8,128)(2,1)S(1)}, u32[]{:S(2)}, u32[]{:S(2)}) collective-permute-start(bf16[384,640]{1,0:T(8,128)(2,1)S(1)} %get-tuple-element.12), channel_id=1, source_target_pairs={{0,20},{1,21},{2,22},{3,23},{4,16},{5,17},{6,18},{7,19},{8,28},{9,... | collective-permute-start | bytes 1474568 | tf_op jit(solution)/shard_map/ppermute | solution.py:27
  15.5 22.2 %collective-permute-start.1 = (bf16[384,640]{1,0:T(8,128)(2,1)S(1)}, bf16[384,640]{1,0:T(8,128)(2,1)S(1)}, u32[]{:S(2)}, u32[]{:S(2)}) collective-permute-start(bf16[384,640]{1,0:T(8,128)(2,1)S(1)} %get-tuple-element.11.refs_0_), channel_id=1, source_target_pairs={{0,8},{1,9},{2,10},{3,11},{4,12},{5,13},{6,14},{7,15},{8,0},{9,1},... | collective-permute-start | bytes 1474568 | tf_op jit(solution)/shard_map/ppermute | solution.py:27
  15.5 29.1 %collective-permute-start = (bf16[384,640]{1,0:T(8,128)(2,1)S(1)}, bf16[384,640]{1,0:T(8,128)(2,1)S(1)}, u32[]{:S(2)}, u32[]{:S(2)}) collective-permute-start(bf16[384,640]{1,0:T(8,128)(2,1)S(1)} %copy-done.4), channel_id=1, source_target_pairs={{0,4},{1,5},{2,6},{3,7},{4,0},{5,1},{6,2},{7,3},{8,12},{9,13},{10,... | collective-permute-start | bytes 1474568 | tf_op jit(solution)/shard_map/ppermute | solution.py:27
  27.0 17.5 %collective-permute-start.3 = (bf16[384,640]{1,0:T(8,128)(2,1)S(1)}, bf16[384,640]{1,0:T(8,128)(2,1)S(1)}, u32[]{:S(2)}, u32[]{:S(2)}) collective-permute-start(bf16[384,640]{1,0:T(8,128)(2,1)S(1)} %collective-permute-done.2.refs_2_), channel_id=1, source_target_pairs={{0,8},{1,9},{2,10},{3,11},{4,12},{5,13},{6,14},{7,15},{8,0},{9,1},... | collective-permute-start | bytes 1474568 | tf_op jit(solution)/shard_map/ppermute | solution.py:27
  37.2 7.4 %collective-permute-start.5 = (bf16[384,640]{1,0:T(8,128)(2,1)S(1)}, bf16[384,640]{1,0:T(8,128)(2,1)S(1)}, u32[]{:S(2)}, u32[]{:S(2)}) collective-permute-start(bf16[384,640]{1,0:T(8,128)(2,1)S(1)} %collective-permute-done.4.refs_4_), channel_id=1, source_target_pairs={{0,8},{1,9},{2,10},{3,11},{4,12},{5,13},{6,14},{7,15},{8,0},{9,1},... | collective-permute-start | bytes 1474568 | tf_op jit(solution)/shard_map/ppermute | solution.py:27
  37.2 7.4 %collective-permute-start.7 = (bf16[384,640]{1,0:T(8,128)(2,1)S(1)}, bf16[384,640]{1,0:T(8,128)(2,1)S(1)}, u32[]{:S(2)}, u32[]{:S(2)}) collective-permute-start(bf16[384,640]{1,0:T(8,128)(2,1)S(1)} %collective-permute-done.6.refs_6_), channel_id=1, source_target_pairs={{0,8},{1,9},{2,10},{3,11},{4,12},{5,13},{6,14},{7,15},{8,0},{9,1},... | collective-permute-start | bytes 1474568 | tf_op jit(solution)/shard_map/ppermute | solution.py:27
  49.1 1.7 %copy-start.1 = (bf16[4,640,640]{2,1,0:T(8,128)(2,1)}, bf16[4,640,640]{2,1,0:T(8,128)(2,1)S(1)}, u32[]{:S(2)}) copy-start(bf16[4,640,640]{2,1,0:T(8,128)(2,1)S(1)} %shard_map.59) | copy-start | bytes 9830404
  50.7 0.8 copy-start.5
  51.5 0.8 copy-start.7
  52.3 0.8 copy-start.9
  53.1 0.8 copy-start.11
  53.9 0.8 copy-start.13
  59.0 1.9 %copy-start.3 = (bf16[2560,640]{1,0:T(8,128)(2,1)S(1)}, bf16[2560,640]{1,0:T(8,128)(2,1)}, u32[]{:S(2)}) copy-start(bf16[2560,640]{1,0:T(8,128)(2,1)} %all-gather.2.cloned.1.call-done) | copy-start | bytes 9830404
  60.9 4.7 %copy-start.6 = (bf16[384,640]{1,0:T(8,128)(2,1)S(1)}, bf16[384,640]{1,0:T(8,128)(2,1)}, u32[]{:S(2)}) copy-start(bf16[384,640]{1,0:T(8,128)(2,1)} %copy-done.5) | copy-start | bytes 1474564
  60.9 4.7 %copy-start.8 = (bf16[384,640]{1,0:T(8,128)(2,1)S(1)}, bf16[384,640]{1,0:T(8,128)(2,1)}, u32[]{:S(2)}) copy-start(bf16[384,640]{1,0:T(8,128)(2,1)} %copy-done.7) | copy-start | bytes 1474564
  60.9 4.7 %copy-start.10 = (bf16[384,640]{1,0:T(8,128)(2,1)S(1)}, bf16[384,640]{1,0:T(8,128)(2,1)}, u32[]{:S(2)}) copy-start(bf16[384,640]{1,0:T(8,128)(2,1)} %copy-done.9) | copy-start | bytes 1474564
  60.9 4.7 %copy-start.12 = (bf16[384,640]{1,0:T(8,128)(2,1)S(1)}, bf16[384,640]{1,0:T(8,128)(2,1)}, u32[]{:S(2)}) copy-start(bf16[384,640]{1,0:T(8,128)(2,1)} %copy-done.11) | copy-start | bytes 1474564
  60.9 4.7 %copy-start.14 = (bf16[384,640]{1,0:T(8,128)(2,1)S(1)}, bf16[384,640]{1,0:T(8,128)(2,1)}, u32[]{:S(2)}) copy-start(bf16[384,640]{1,0:T(8,128)(2,1)} %copy-done.13) | copy-start | bytes 1474564
  65.3 5.5 %collective-permute-start.8 = (bf16[2,2,384,640]{3,2,1,0:T(8,128)(2,1)S(1)}, bf16[2,2,384,640]{3,2,1,0:T(8,128)(2,1)S(1)}, u32[]{:S(2)}, u32[]{:S(2)}) collective-permute-start(bf16[2,2,384,640]{3,2,1,0:T(8,128)(2,1)S(1)} %get-tuple-element.15), channel_id=1, source_target_pairs={{0,8},{1,9},{2,10},{3,11},{4,12},{5,13},{6,14},{7,15},{8,0},{9,1},... | collective-permute-start | bytes 5898248 | tf_op jit(solution)/shard_map/ppermute | solution.py:27
  69.8 40.2 %collective-permute-start.12 = (bf16[384,640]{1,0:T(8,128)(2,1)}, bf16[384,640]{1,0:T(8,128)(2,1)}, u32[]{:S(2)}, u32[]{:S(2)}) collective-permute-start(bf16[384,640]{1,0:T(8,128)(2,1)} %get-tuple-element.17), channel_id=1, source_target_pairs={{0,4},{1,5},{2,6},{3,7},{4,0},{5,1},{6,2},{7,3},{8,12},{9,13},{10,... | collective-permute-start | bytes 1474568 | tf_op jit(solution)/shard_map/ppermute | solution.py:27
  72.4 39.4 %collective-permute-start.10 = (bf16[384,640]{1,0:T(8,128)(2,1)}, bf16[384,640]{1,0:T(8,128)(2,1)}, u32[]{:S(2)}, u32[]{:S(2)}) collective-permute-start(bf16[384,640]{1,0:T(8,128)(2,1)} %get-tuple-element.20), channel_id=1, source_target_pairs={{0,4},{1,5},{2,6},{3,7},{4,0},{5,1},{6,2},{7,3},{8,12},{9,13},{10,... | collective-permute-start | bytes 1474568 | tf_op jit(solution)/shard_map/ppermute | solution.py:27
  73.6 42.0 %collective-permute-start.11 = (bf16[384,640]{1,0:T(8,128)(2,1)}, bf16[384,640]{1,0:T(8,128)(2,1)}, u32[]{:S(2)}, u32[]{:S(2)}) collective-permute-start(bf16[384,640]{1,0:T(8,128)(2,1)} %get-tuple-element.19), channel_id=1, source_target_pairs={{0,20},{1,21},{2,22},{3,23},{4,16},{5,17},{6,18},{7,19},{8,28},{9,... | collective-permute-start | bytes 1474568 | tf_op jit(solution)/shard_map/ppermute | solution.py:27
  74.1 41.4 %collective-permute-start.9 = (bf16[384,640]{1,0:T(8,128)(2,1)}, bf16[384,640]{1,0:T(8,128)(2,1)}, u32[]{:S(2)}, u32[]{:S(2)}) collective-permute-start(bf16[384,640]{1,0:T(8,128)(2,1)} %get-tuple-element.21), channel_id=1, source_target_pairs={{0,16},{1,17},{2,18},{3,19},{4,20},{5,21},{6,22},{7,23},{8,24},{9,... | collective-permute-start | bytes 1474568 | tf_op jit(solution)/shard_map/ppermute | solution.py:27
  108.5 9.9 %collective-permute-start.13 = (bf16[80,640]{1,0:T(8,128)(2,1)S(1)}, bf16[80,640]{1,0:T(8,128)(2,1)S(1)}, u32[]{:S(2)}, u32[]{:S(2)}) collective-permute-start(bf16[80,640]{1,0:T(8,128)(2,1)S(1)} %get-tuple-element.22), channel_id=1, source_target_pairs={{0,1},{1,2},{2,3},{3,0},{4,5},{5,6},{6,7},{7,4},{8,9},{9,10},{10,1... | collective-permute-start | bytes 307208 | tf_op jit(solution)/shard_map/ppermute | solution.py:27
  110.1 8.3 %collective-permute-start.14 = (bf16[80,640]{1,0:T(8,128)(2,1)S(1)}, bf16[80,640]{1,0:T(8,128)(2,1)S(1)}, u32[]{:S(2)}, u32[]{:S(2)}) collective-permute-start(bf16[80,640]{1,0:T(8,128)(2,1)S(1)} %get-tuple-element.24), channel_id=1, source_target_pairs={{0,3},{1,0},{2,1},{3,2},{4,7},{5,4},{6,5},{7,6},{8,11},{9,8},{10,9... | collective-permute-start | bytes 307208 | tf_op jit(solution)/shard_map/ppermute | solution.py:27
  111.8 6.6 %collective-permute-start.15 = (bf16[80,640]{1,0:T(8,128)(2,1)S(1)}, bf16[80,640]{1,0:T(8,128)(2,1)S(1)}, u32[]{:S(2)}, u32[]{:S(2)}) collective-permute-start(bf16[80,640]{1,0:T(8,128)(2,1)S(1)} %get-tuple-element.23), channel_id=1, source_target_pairs={{0,2},{1,3},{2,0},{3,1},{4,6},{5,7},{6,4},{7,5},{8,10},{9,11},{10,... | collective-permute-start | bytes 307208 | tf_op jit(solution)/shard_map/ppermute | solution.py:27
Sparse Core Ops, SparseCore 0:
  9.8 49.1 all-gather.1
  61.5 45.9 reduce-scatter.1

commit v4 on v3

--- a/solution.py
+++ b/solution.py
@@ -63,7 +63,9 @@
 
 
 def over_y(v, y):
-    return add(pick(v, y, 0), *(to_y(pick(v, (y + d) % 4, 0), d) for d in (1, 3, 2)))
+    turn = (1, 3, 2)
+    mine, *pieces = lax.optimization_barrier([pick(v, (y + d) % 4, 0) for d in (0, *turn)])
+    return add(mine, *(to_y(piece, d) for piece, d in zip(pieces, turn)))
 
 
 def call(kernel, outs, flops, n_in):

time: 127 us -> 126 us (level)
  no operation moved by 1% of the time
where the time goes in v4:
time: 126 us
  waiting for transfers between devices  63 us (50%)
  Pallas kernels  16.7 us (13%)
  starting transfers between devices  16 us (13%)
  between operations  14.2 us (11%)
  local copies, waits for them, and re-layouts  12.9 us (10%)
  other arithmetic  3.21 us (3%)
    reduce_scatter x1, waiting for transfers between devices, body(): lax.psum_scatter(gw.reshape(8, 4, 80, 640), 'blk', scatter_dimension=0, t...  31 us
    ppermute x16, waiting for transfers between devices, move(): lax.ppermute(value, ALL, [(number(*p), number(*target(*p))) for p in plac...  27.7 us
    ppermute x16, starting transfers between devices, move(): lax.ppermute(value, ALL, [(number(*p), number(*target(*p))) for p in plac...  15.9 us
    unnamed x30, local copies, waits for them, and re-layouts  9.85 us
    pallas_call x1, Pallas kernels, body(): call(gw_kernel, [(4, 640, 640)], WORK, 10)(at, *own, *far, context, c_far)  4.5 us
    pallas_call x1, Pallas kernels, body(): call(proj_kernel, [(2, 2, 384, 640)] * 2, WORK, 3)(at, context, c_far, w)  4.35 us
    all_gather x1, waiting for transfers between devices, body(): weight = lax.all_gather(half, 'blk', axis=0, tiled=True)  4.25 us
    pallas_call x1, Pallas kernels, body(): call(gc_kernel, [(384, 640)] * 2, WORK, 9)(at, *own, *far, w)  4.2 us
  transfers between devices with their start and end apart: 18, of which 5 were waited for; matrix products, arithmetic and copies ran while one was open for 4% of the time, Pallas kernels for 13%

profile of v4, /device:TPU:6, one launch (start us, length us, event | category | flops | bytes accessed | tf_op | source)
XLA Modules:
  0.0 126.0 jit_solution(6570417801900561827)
XLA Ops:
  7.2 0.0 copy-start
  7.2 0.0 all-gather.2.cloned.1.call-start
  7.3 1.1 copy-done
  8.3 0.8 constant_dynamic-slice_fusion
  9.1 0.0 all-gather.2.cloned.1.call-update
  9.1 0.0 reduce-scatter.2.cloned.1.call-start
  9.2 0.1 pad_add_fusion.at
  9.3 1.2 copy-done.2
  10.5 0.8 shard_map.58
  11.3 1.5 %collective-permute-start.2 = (bf16[384,640]{1,0:T(8,128)(2,1)S(1)}, bf16[384,640]{1,0:T(8,128)(2,1)S(1)}, u32[]{:S(2)}, u32[]{:S(2)}) collective-permute-start(bf16[384,640]{1,0:T(8,128)(2,1)S(1)} %get-tuple-element.15.refs_0_), channel_id=1, source_target_pairs={{0,16},{1,17},{2,18},{3,19},{4,20},{5,21},{6,22},{7,23},{8,24},{9,... | collective-permute-start | bytes 1474568 | tf_op jit(solution)/shard_map/ppermute | solution.py:27
  12.8 1.7 %collective-permute-start.4 = (bf16[384,640]{1,0:T(8,128)(2,1)S(1)}, bf16[384,640]{1,0:T(8,128)(2,1)S(1)}, u32[]{:S(2)}, u32[]{:S(2)}) collective-permute-start(bf16[384,640]{1,0:T(8,128)(2,1)S(1)} %get-tuple-element.16), channel_id=1, source_target_pairs={{0,4},{1,5},{2,6},{3,7},{4,0},{5,1},{6,2},{7,3},{8,12},{9,13},{10,... | collective-permute-start | bytes 1474568 | tf_op jit(solution)/shard_map/ppermute | solution.py:27
  14.5 1.0 collective-permute-start.6
  15.5 0.0 collective-permute-start.1
  15.5 0.8 collective-permute-start
  16.3 10.7 %collective-permute-done.2.refs_2_ = bf16[384,640]{1,0:T(8,128)(2,1)S(1)} collective-permute-done((bf16[384,640]{1,0:T(8,128)(2,1)S(1)}, bf16[384,640]{1,0:T(8,128)(2,1)S(1)}, u32[]{:S(2)}, u32[]{:S(2)}) %collective-permute-start.2) | collective-permute-done | bytes 491552 | tf_op jit(solution)/shard_map/ppermute | solution.py:27
  27.0 0.0 collective-permute-start.3
  27.0 10.1 %collective-permute-done.4.refs_4_ = bf16[384,640]{1,0:T(8,128)(2,1)S(1)} collective-permute-done((bf16[384,640]{1,0:T(8,128)(2,1)S(1)}, bf16[384,640]{1,0:T(8,128)(2,1)S(1)}, u32[]{:S(2)}, u32[]{:S(2)}) %collective-permute-start.4) | collective-permute-done | bytes 491552 | tf_op jit(solution)/shard_map/ppermute | solution.py:27
  37.2 0.0 collective-permute-done.6.refs_6_
  37.2 0.5 collective-permute-start.7
  37.7 0.0 collective-permute-done.1.refs_1_
  37.7 6.9 %collective-permute-done.refs_9_.c_far = bf16[384,640]{1,0:T(8,128)(2,1)S(1)} collective-permute-done((bf16[384,640]{1,0:T(8,128)(2,1)S(1)}, bf16[384,640]{1,0:T(8,128)(2,1)S(1)}, u32[]{:S(2)}, u32[]{:S(2)}) %collective-permute-start) | collective-permute-done | bytes 491552 | tf_op jit(solution)/shard_map/ppermute | solution.py:27
  44.6 4.5 %shard_map.59 = bf16[4,640,640]{2,1,0:T(8,128)(2,1)S(1)} custom-call(s32[2]{0:T(128)S(1)} %pad_add_fusion.at, bf16[384,640]{1,0:T(8,128)(2,1)S(1)} %get-tuple-element.15.refs_0_, bf16[384,640]{1,0:T(8,128)(2,1)S(1)} %collective-permute-done.1.refs_1_, bf16[384,640]{1,0:T(8,128)(2,1)S(1)} %collective-permute-done.2.refs_2_, ...), custom_call_target="tpu_custom_call" | custom-call | flops 2516582400 | bytes 8388608 | tf_op jit(solution)/shard_map/pallas_call | solution.py:143
  49.1 1.7 %copy-done.1 = bf16[4,640,640]{2,1,0:T(8,128)(2,1)} copy-done((bf16[4,640,640]{2,1,0:T(8,128)(2,1)}, bf16[4,640,640]{2,1,0:T(8,128)(2,1)S(1)}, u32[]{:S(2)}) %copy-start.1) | copy-done | bytes 3276824
  50.8 0.8 copy-done.5
  51.5 0.8 copy-done.7
  52.3 0.8 copy-done.9
  53.1 0.8 copy-done.11
  53.9 0.8 copy-done.13
  54.7 4.2 %all-gather.2.cloned.1.call-done = bf16[2560,640]{1,0:T(8,128)(2,1)} async-done(((bf16[320,640]{1,0:T(8,128)(2,1)}), bf16[2560,640]{1,0:T(8,128)(2,1)}) %all-gather.2.cloned.1.call-update) | async-done | bytes 3276816 | tf_op jit(solution)/shard_map/all_gather | solution.py:133
  59.0 0.0 reduce-scatter.2.cloned.1.call-update
  59.0 1.9 %copy-done.3 = bf16[2560,640]{1,0:T(8,128)(2,1)S(1)} copy-done((bf16[2560,640]{1,0:T(8,128)(2,1)S(1)}, bf16[2560,640]{1,0:T(8,128)(2,1)}, u32[]{:S(2)}) %copy-start.3) | copy-done | bytes 3276824
  60.9 4.4 %shard_map.60 = (bf16[2,2,384,640]{3,2,1,0:T(8,128)(2,1)S(1)}, bf16[2,2,384,640]{3,2,1,0:T(8,128)(2,1)S(1)}) custom-call(s32[2]{0:T(128)S(1)} %pad_add_fusion.at, bf16[384,640]{1,0:T(8,128)(2,1)S(1)} %copy-done.4, bf16[384,640]{1,0:T(8,128)(2,1)S(1)} %collective-permute-done.refs_9_.c_far, bf16[4,640,640]{2,1,0:T(8,128)(2,1)S(1)} %bitcast.19), custom_call_target="tpu_custom_call" | custom-call | flops 2516582400 | bytes 8388608 | tf_op jit(solution)/shard_map/pallas_call | solution.py:149
  65.3 0.3 collective-permute-start.8
  65.6 4.2 %shard_map.62 = (bf16[384,640]{1,0:T(8,128)(2,1)}, bf16[384,640]{1,0:T(8,128)(2,1)S(1)}) custom-call(s32[2]{0:T(128)S(1)} %pad_add_fusion.at, bf16[384,640]{1,0:T(8,128)(2,1)S(1)} %get-tuple-element.15.refs_0_, bf16[384,640]{1,0:T(8,128)(2,1)S(1)} %copy-done.8, bf16[384,640]{1,0:T(8,128)(2,1)S(1)} %collective-permute-done.2.refs_2_, ...), custom_call_target="tpu_custom_call" | custom-call | flops 2516582400 | bytes 8388608 | tf_op jit(solution)/shard_map/pallas_call | solution.py:154
  69.8 0.9 collective-permute-start.12
  70.8 0.5 add_convert_fusion.keep
  71.3 1.1 slice_bitcast_fusion
  72.4 1.2 collective-permute-start.10
  73.6 0.5 collective-permute-start.11
  74.1 2.4 %collective-permute-start.9 = (bf16[384,640]{1,0:T(8,128)(2,1)}, bf16[384,640]{1,0:T(8,128)(2,1)}, u32[]{:S(2)}, u32[]{:S(2)}) collective-permute-start(bf16[384,640]{1,0:T(8,128)(2,1)} %get-tuple-element.29), channel_id=1, source_target_pairs={{0,16},{1,17},{2,18},{3,19},{4,20},{5,21},{6,22},{7,23},{8,24},{9,... | collective-permute-start | bytes 1474568 | tf_op jit(solution)/shard_map/ppermute | solution.py:27
  76.5 31.0 %reduce-scatter.2.cloned.1.call-done = bf16[1,4,80,640]{3,2,1,0:T(8,128)(2,1)} async-done(((bf16[8,4,80,640]{3,2,1,0:T(8,128)(2,1)}), bf16[1,4,80,640]{3,2,1,0:T(8,128)(2,1)}) %reduce-scatter.2.cloned.1.call-update) | async-done | bytes 409616 | tf_op jit(solution)/shard_map/reduce_scatter | solution.py:145
  107.5 1.1 dynamic-slice_bitcast_fusion
  108.6 1.6 %collective-permute-start.13 = (bf16[80,640]{1,0:T(8,128)(2,1)S(1)}, bf16[80,640]{1,0:T(8,128)(2,1)S(1)}, u32[]{:S(2)}, u32[]{:S(2)}) collective-permute-start(bf16[80,640]{1,0:T(8,128)(2,1)S(1)} %get-tuple-element.24), channel_id=1, source_target_pairs={{0,1},{1,2},{2,3},{3,0},{4,5},{5,6},{6,7},{7,4},{8,9},{9,10},{10,1... | collective-permute-start | bytes 307208 | tf_op jit(solution)/shard_map/ppermute | solution.py:27
  110.1 1.8 %collective-permute-start.14 = (bf16[80,640]{1,0:T(8,128)(2,1)S(1)}, bf16[80,640]{1,0:T(8,128)(2,1)S(1)}, u32[]{:S(2)}, u32[]{:S(2)}) collective-permute-start(bf16[80,640]{1,0:T(8,128)(2,1)S(1)} %get-tuple-element.25), channel_id=1, source_target_pairs={{0,3},{1,0},{2,1},{3,2},{4,7},{5,4},{6,5},{7,6},{8,11},{9,8},{10,9... | collective-permute-start | bytes 307208 | tf_op jit(solution)/shard_map/ppermute | solution.py:27
  111.9 1.8 %collective-permute-start.15 = (bf16[80,640]{1,0:T(8,128)(2,1)S(1)}, bf16[80,640]{1,0:T(8,128)(2,1)S(1)}, u32[]{:S(2)}, u32[]{:S(2)}) collective-permute-start(bf16[80,640]{1,0:T(8,128)(2,1)S(1)} %get-tuple-element.26), channel_id=1, source_target_pairs={{0,2},{1,3},{2,0},{3,1},{4,6},{5,7},{6,4},{7,5},{8,10},{9,11},{10,... | collective-permute-start | bytes 307208 | tf_op jit(solution)/shard_map/ppermute | solution.py:27
  113.7 1.9 %add_convert_fusion.1 = bf16[384,640]{1,0:T(8,128)(2,1)} fusion(bf16[384,640]{1,0:T(8,128)(2,1)} %collective-permute-done.12, bf16[384,640]{1,0:T(8,128)(2,1)S(1)} %get-tuple-element.20), kind=kLoop, calls=%fused_computation.1 | loop fusion | flops 983040 | bytes 1474560 | tf_op jit(solution)/shard_map/convert_element_type | solution.py:155
  115.6 2.8 %shard_map.61 = bf16[384,1280]{1,0:T(8,128)(2,1)} custom-call(s32[2]{0:T(128)S(1)} %pad_add_fusion.at, bf16[2,2,384,640]{3,2,1,0:T(8,128)(2,1)S(1)} %add_convert_fusion.keep, bf16[384,640]{1,0:T(8,128)(2,1)} %collective-permute-done.9.hi, bf16[384,640]{1,0:T(8,128)(2,1)} %collective-permute-done.10.lo, bf16[384,640]{1,0:T(8,128)(2,1)} %collective-permute-done.11.both), custom_call_target="tpu_custom_call" | custom-call | bytes 8388608 | tf_op jit(solution)/shard_map/pallas_call | solution.py:152
  118.5 0.7 convert_add_fusion
  (32 shorter events, 0.1 us)
Async XLA Ops:
  7.2 1.2 copy-start
  7.2 8.3 %copy-start.4 = (bf16[384,640]{1,0:T(8,128)(2,1)S(1)}, bf16[384,640]{1,0:T(8,128)(2,1)}, u32[]{:S(2)}) copy-start(bf16[384,640]{1,0:T(8,128)(2,1)} %c_own.1) | copy-start | bytes 1474564
  7.2 51.8 %all-gather.2.cloned.1.call-start = ((), (), s32[]{:S(2)}) async-start(), calls=%async_computation.1 | async-start | bytes 3686400 | tf_op jit(solution)/shard_map/all_gather | solution.py:133
  9.1 98.3 %reduce-scatter.2.cloned.1.call-start = ((), (), s32[]{:S(2)}) async-start(), calls=%async_computation.2 | async-start | bytes 3686400 | tf_op jit(solution)/shard_map/reduce_scatter | solution.py:145
  9.3 1.2 copy-start.2
  11.3 15.7 %collective-permute-start.2 = (bf16[384,640]{1,0:T(8,128)(2,1)S(1)}, bf16[384,640]{1,0:T(8,128)(2,1)S(1)}, u32[]{:S(2)}, u32[]{:S(2)}) collective-permute-start(bf16[384,640]{1,0:T(8,128)(2,1)S(1)} %get-tuple-element.15.refs_0_), channel_id=1, source_target_pairs={{0,16},{1,17},{2,18},{3,19},{4,20},{5,21},{6,22},{7,23},{8,24},{9,... | collective-permute-start | bytes 1474568 | tf_op jit(solution)/shard_map/ppermute | solution.py:27
  12.8 24.4 %collective-permute-start.4 = (bf16[384,640]{1,0:T(8,128)(2,1)S(1)}, bf16[384,640]{1,0:T(8,128)(2,1)S(1)}, u32[]{:S(2)}, u32[]{:S(2)}) collective-permute-start(bf16[384,640]{1,0:T(8,128)(2,1)S(1)} %get-tuple-element.16), channel_id=1, source_target_pairs={{0,4},{1,5},{2,6},{3,7},{4,0},{5,1},{6,2},{7,3},{8,12},{9,13},{10,... | collective-permute-start | bytes 1474568 | tf_op jit(solution)/shard_map/ppermute | solution.py:27
  14.5 22.7 %collective-permute-start.6 = (bf16[384,640]{1,0:T(8,128)(2,1)S(1)}, bf16[384,640]{1,0:T(8,128)(2,1)S(1)}, u32[]{:S(2)}, u32[]{:S(2)}) collective-permute-start(bf16[384,640]{1,0:T(8,128)(2,1)S(1)} %get-tuple-element.16), channel_id=1, source_target_pairs={{0,20},{1,21},{2,22},{3,23},{4,16},{5,17},{6,18},{7,19},{8,28},{9,... | collective-permute-start | bytes 1474568 | tf_op jit(solution)/shard_map/ppermute | solution.py:27
  15.5 22.2 %collective-permute-start.1 = (bf16[384,640]{1,0:T(8,128)(2,1)S(1)}, bf16[384,640]{1,0:T(8,128)(2,1)S(1)}, u32[]{:S(2)}, u32[]{:S(2)}) collective-permute-start(bf16[384,640]{1,0:T(8,128)(2,1)S(1)} %get-tuple-element.15.refs_0_), channel_id=1, source_target_pairs={{0,8},{1,9},{2,10},{3,11},{4,12},{5,13},{6,14},{7,15},{8,0},{9,1},... | collective-permute-start | bytes 1474568 | tf_op jit(solution)/shard_map/ppermute | solution.py:27
  15.5 29.1 %collective-permute-start = (bf16[384,640]{1,0:T(8,128)(2,1)S(1)}, bf16[384,640]{1,0:T(8,128)(2,1)S(1)}, u32[]{:S(2)}, u32[]{:S(2)}) collective-permute-start(bf16[384,640]{1,0:T(8,128)(2,1)S(1)} %copy-done.4), channel_id=1, source_target_pairs={{0,4},{1,5},{2,6},{3,7},{4,0},{5,1},{6,2},{7,3},{8,12},{9,13},{10,... | collective-permute-start | bytes 1474568 | tf_op jit(solution)/shard_map/ppermute | solution.py:27
  27.0 17.5 %collective-permute-start.3 = (bf16[384,640]{1,0:T(8,128)(2,1)S(1)}, bf16[384,640]{1,0:T(8,128)(2,1)S(1)}, u32[]{:S(2)}, u32[]{:S(2)}) collective-permute-start(bf16[384,640]{1,0:T(8,128)(2,1)S(1)} %collective-permute-done.2.refs_2_), channel_id=1, source_target_pairs={{0,8},{1,9},{2,10},{3,11},{4,12},{5,13},{6,14},{7,15},{8,0},{9,1},... | collective-permute-start | bytes 1474568 | tf_op jit(solution)/shard_map/ppermute | solution.py:27
  37.2 7.4 %collective-permute-start.5 = (bf16[384,640]{1,0:T(8,128)(2,1)S(1)}, bf16[384,640]{1,0:T(8,128)(2,1)S(1)}, u32[]{:S(2)}, u32[]{:S(2)}) collective-permute-start(bf16[384,640]{1,0:T(8,128)(2,1)S(1)} %collective-permute-done.4.refs_4_), channel_id=1, source_target_pairs={{0,8},{1,9},{2,10},{3,11},{4,12},{5,13},{6,14},{7,15},{8,0},{9,1},... | collective-permute-start | bytes 1474568 | tf_op jit(solution)/shard_map/ppermute | solution.py:27
  37.2 7.4 %collective-permute-start.7 = (bf16[384,640]{1,0:T(8,128)(2,1)S(1)}, bf16[384,640]{1,0:T(8,128)(2,1)S(1)}, u32[]{:S(2)}, u32[]{:S(2)}) collective-permute-start(bf16[384,640]{1,0:T(8,128)(2,1)S(1)} %collective-permute-done.6.refs_6_), channel_id=1, source_target_pairs={{0,8},{1,9},{2,10},{3,11},{4,12},{5,13},{6,14},{7,15},{8,0},{9,1},... | collective-permute-start | bytes 1474568 | tf_op jit(solution)/shard_map/ppermute | solution.py:27
  49.1 1.7 %copy-start.1 = (bf16[4,640,640]{2,1,0:T(8,128)(2,1)}, bf16[4,640,640]{2,1,0:T(8,128)(2,1)S(1)}, u32[]{:S(2)}) copy-start(bf16[4,640,640]{2,1,0:T(8,128)(2,1)S(1)} %shard_map.59) | copy-start | bytes 9830404
  50.7 0.8 copy-start.5
  51.5 0.8 copy-start.7
  52.3 0.8 copy-start.9
  53.1 0.8 copy-start.11
  53.9 0.8 copy-start.13
  59.0 1.9 %copy-start.3 = (bf16[2560,640]{1,0:T(8,128)(2,1)S(1)}, bf16[2560,640]{1,0:T(8,128)(2,1)}, u32[]{:S(2)}) copy-start(bf16[2560,640]{1,0:T(8,128)(2,1)} %all-gather.2.cloned.1.call-done) | copy-start | bytes 9830404
  60.9 4.7 %copy-start.6 = (bf16[384,640]{1,0:T(8,128)(2,1)S(1)}, bf16[384,640]{1,0:T(8,128)(2,1)}, u32[]{:S(2)}) copy-start(bf16[384,640]{1,0:T(8,128)(2,1)} %copy-done.5) | copy-start | bytes 1474564
  60.9 4.7 %copy-start.8 = (bf16[384,640]{1,0:T(8,128)(2,1)S(1)}, bf16[384,640]{1,0:T(8,128)(2,1)}, u32[]{:S(2)}) copy-start(bf16[384,640]{1,0:T(8,128)(2,1)} %copy-done.7) | copy-start | bytes 1474564
  60.9 4.7 %copy-start.10 = (bf16[384,640]{1,0:T(8,128)(2,1)S(1)}, bf16[384,640]{1,0:T(8,128)(2,1)}, u32[]{:S(2)}) copy-start(bf16[384,640]{1,0:T(8,128)(2,1)} %copy-done.9) | copy-start | bytes 1474564
  60.9 4.7 %copy-start.12 = (bf16[384,640]{1,0:T(8,128)(2,1)S(1)}, bf16[384,640]{1,0:T(8,128)(2,1)}, u32[]{:S(2)}) copy-start(bf16[384,640]{1,0:T(8,128)(2,1)} %copy-done.11) | copy-start | bytes 1474564
  60.9 4.7 %copy-start.14 = (bf16[384,640]{1,0:T(8,128)(2,1)S(1)}, bf16[384,640]{1,0:T(8,128)(2,1)}, u32[]{:S(2)}) copy-start(bf16[384,640]{1,0:T(8,128)(2,1)} %copy-done.13) | copy-start | bytes 1474564
  65.3 5.5 %collective-permute-start.8 = (bf16[2,2,384,640]{3,2,1,0:T(8,128)(2,1)S(1)}, bf16[2,2,384,640]{3,2,1,0:T(8,128)(2,1)S(1)}, u32[]{:S(2)}, u32[]{:S(2)}) collective-permute-start(bf16[2,2,384,640]{3,2,1,0:T(8,128)(2,1)S(1)} %get-tuple-element.19), channel_id=1, source_target_pairs={{0,8},{1,9},{2,10},{3,11},{4,12},{5,13},{6,14},{7,15},{8,0},{9,1},... | collective-permute-start | bytes 5898248 | tf_op jit(solution)/shard_map/ppermute | solution.py:27
  69.8 40.3 %collective-permute-start.12 = (bf16[384,640]{1,0:T(8,128)(2,1)}, bf16[384,640]{1,0:T(8,128)(2,1)}, u32[]{:S(2)}, u32[]{:S(2)}) collective-permute-start(bf16[384,640]{1,0:T(8,128)(2,1)} %get-tuple-element.21), channel_id=1, source_target_pairs={{0,4},{1,5},{2,6},{3,7},{4,0},{5,1},{6,2},{7,3},{8,12},{9,13},{10,... | collective-permute-start | bytes 1474568 | tf_op jit(solution)/shard_map/ppermute | solution.py:27
  72.4 39.5 %collective-permute-start.10 = (bf16[384,640]{1,0:T(8,128)(2,1)}, bf16[384,640]{1,0:T(8,128)(2,1)}, u32[]{:S(2)}, u32[]{:S(2)}) collective-permute-start(bf16[384,640]{1,0:T(8,128)(2,1)} %get-tuple-element.28), channel_id=1, source_target_pairs={{0,4},{1,5},{2,6},{3,7},{4,0},{5,1},{6,2},{7,3},{8,12},{9,13},{10,... | collective-permute-start | bytes 1474568 | tf_op jit(solution)/shard_map/ppermute | solution.py:27
  73.6 42.0 %collective-permute-start.11 = (bf16[384,640]{1,0:T(8,128)(2,1)}, bf16[384,640]{1,0:T(8,128)(2,1)}, u32[]{:S(2)}, u32[]{:S(2)}) collective-permute-start(bf16[384,640]{1,0:T(8,128)(2,1)} %get-tuple-element.27), channel_id=1, source_target_pairs={{0,20},{1,21},{2,22},{3,23},{4,16},{5,17},{6,18},{7,19},{8,28},{9,... | collective-permute-start | bytes 1474568 | tf_op jit(solution)/shard_map/ppermute | solution.py:27
  74.1 41.5 %collective-permute-start.9 = (bf16[384,640]{1,0:T(8,128)(2,1)}, bf16[384,640]{1,0:T(8,128)(2,1)}, u32[]{:S(2)}, u32[]{:S(2)}) collective-permute-start(bf16[384,640]{1,0:T(8,128)(2,1)} %get-tuple-element.29), channel_id=1, source_target_pairs={{0,16},{1,17},{2,18},{3,19},{4,20},{5,21},{6,22},{7,23},{8,24},{9,... | collective-permute-start | bytes 1474568 | tf_op jit(solution)/shard_map/ppermute | solution.py:27
  108.6 9.9 %collective-permute-start.13 = (bf16[80,640]{1,0:T(8,128)(2,1)S(1)}, bf16[80,640]{1,0:T(8,128)(2,1)S(1)}, u32[]{:S(2)}, u32[]{:S(2)}) collective-permute-start(bf16[80,640]{1,0:T(8,128)(2,1)S(1)} %get-tuple-element.24), channel_id=1, source_target_pairs={{0,1},{1,2},{2,3},{3,0},{4,5},{5,6},{6,7},{7,4},{8,9},{9,10},{10,1... | collective-permute-start | bytes 307208 | tf_op jit(solution)/shard_map/ppermute | solution.py:27
  110.1 8.3 %collective-permute-start.14 = (bf16[80,640]{1,0:T(8,128)(2,1)S(1)}, bf16[80,640]{1,0:T(8,128)(2,1)S(1)}, u32[]{:S(2)}, u32[]{:S(2)}) collective-permute-start(bf16[80,640]{1,0:T(8,128)(2,1)S(1)} %get-tuple-element.25), channel_id=1, source_target_pairs={{0,3},{1,0},{2,1},{3,2},{4,7},{5,4},{6,5},{7,6},{8,11},{9,8},{10,9... | collective-permute-start | bytes 307208 | tf_op jit(solution)/shard_map/ppermute | solution.py:27
  111.9 6.6 %collective-permute-start.15 = (bf16[80,640]{1,0:T(8,128)(2,1)S(1)}, bf16[80,640]{1,0:T(8,128)(2,1)S(1)}, u32[]{:S(2)}, u32[]{:S(2)}) collective-permute-start(bf16[80,640]{1,0:T(8,128)(2,1)S(1)} %get-tuple-element.26), channel_id=1, source_target_pairs={{0,2},{1,3},{2,0},{3,1},{4,6},{5,7},{6,4},{7,5},{8,10},{9,11},{10,... | collective-permute-start | bytes 307208 | tf_op jit(solution)/shard_map/ppermute | solution.py:27
Sparse Core Ops, SparseCore 0:
  9.8 49.1 all-gather.1
  61.5 45.9 reduce-scatter.1

commit v5 on v4

--- a/solution.py
+++ b/solution.py
@@ -143,7 +143,6 @@
     gw = call(gw_kernel, [(4, 640, 640)], WORK, 10)(at, *own, *far, context, c_far)[0]
     gw, weight = lax.optimization_barrier((gw, weight))
     gw = lax.psum_scatter(gw.reshape(8, 4, 80, 640), "blk", scatter_dimension=0, tiled=True)
-    grad_weight = over_y(gw[0], y)
 
     w = weight.reshape(4, 640, 640)
     keep, give = call(proj_kernel, [(2, 2, 384, 640)] * 2, WORK, 3)(at, context, c_far, w)
@@ -153,6 +152,8 @@
 
     gc_far, gc_own = call(gc_kernel, [(384, 640)] * 2, WORK, 9)(at, *own, *far, w)
     grad_context = add(gc_own, swap_lo(gc_far)).astype(BF)
+    gw, grad_context = lax.optimization_barrier((gw[0], grad_context))
+    grad_weight = over_y(gw, y)
     return projected, grad_context, grad_weight
 
 

time: 126 us -> 126 us (level)
  waiting for transfers between devices: 63 us -> 61.3 us
    reduce_scatter x1, waiting for transfers between devices: 31 us -> 20 us  [body(): lax.psum_scatter(gw.reshape(8, 4, 80, 640), 'blk', scatter_dimension=0, t...]
    ppermute x16, waiting for transfers between devices: 27.7 us -> 37 us  [move(): lax.ppermute(value, ALL, [(number(*p), number(*target(*p))) for p in plac...]
    unnamed x30 -> x32, local copies, waits for them, and re-layouts: 9.85 us -> 10.9 us
  transfers between devices with their start and end apart: 18 -> 18, of which waited for: 5 -> 7; matrix products, arithmetic and copies ran while one was open for 4% -> 4% of each run, Pallas kernels for 13% -> 13%
where the time goes in v5:
time: 126 us; the launch traced here: 125 us
  waiting for transfers between devices  61.3 us (49%)
  Pallas kernels  16.5 us (13%)
  starting transfers between devices  16.1 us (13%)
  between operations  14.2 us (11%)
  local copies, waits for them, and re-layouts  13.9 us (11%)
  other arithmetic  3.4 us (3%)
    ppermute x16, waiting for transfers between devices, move(): lax.ppermute(value, ALL, [(number(*p), number(*target(*p))) for p in plac...  37 us
    reduce_scatter x1, waiting for transfers between devices, body(): lax.psum_scatter(gw.reshape(8, 4, 80, 640), 'blk', scatter_dimension=0, t...  20 us
    ppermute x16, starting transfers between devices, move(): lax.ppermute(value, ALL, [(number(*p), number(*target(*p))) for p in plac...  16 us
    unnamed x32, local copies, waits for them, and re-layouts  10.9 us
    pallas_call x1, Pallas kernels, body(): call(gw_kernel, [(4, 640, 640)], WORK, 10)(at, *own, *far, context, c_far)  4.51 us
    pallas_call x1, Pallas kernels, body(): call(proj_kernel, [(2, 2, 384, 640)] * 2, WORK, 3)(at, context, c_far, w)  4.3 us
    all_gather x1, waiting for transfers between devices, body(): weight = lax.all_gather(half, 'blk', axis=0, tiled=True)  4.23 us
    pallas_call x1, Pallas kernels, body(): call(gc_kernel, [(384, 640)] * 2, WORK, 9)(at, *own, *far, w)  4.2 us
  transfers between devices with their start and end apart: 18, of which 7 were waited for; matrix products, arithmetic and copies ran while one was open for 4% of the time, Pallas kernels for 13%

profile of v5, /device:TPU:6, one launch (start us, length us, event | category | flops | bytes accessed | tf_op | source)
XLA Modules:
  0.0 125.4 jit_solution(3816021835580462083)
XLA Ops:
  7.2 0.0 copy-start
  7.2 0.0 all-gather.2.cloned.1.call-start
  7.3 1.1 copy-done
  8.3 0.8 constant_dynamic-slice_fusion
  9.1 0.0 all-gather.2.cloned.1.call-update
  9.2 0.0 reduce-scatter.2.cloned.1.call-start
  9.2 0.1 pad_add_fusion.at
  9.3 1.2 copy-done.2
  10.5 0.8 shard_map.58
  11.3 1.5 %collective-permute-start.2 = (bf16[384,640]{1,0:T(8,128)(2,1)S(1)}, bf16[384,640]{1,0:T(8,128)(2,1)S(1)}, u32[]{:S(2)}, u32[]{:S(2)}) collective-permute-start(bf16[384,640]{1,0:T(8,128)(2,1)S(1)} %get-tuple-element.17.refs_0_), channel_id=1, source_target_pairs={{0,16},{1,17},{2,18},{3,19},{4,20},{5,21},{6,22},{7,23},{8,24},{9,... | collective-permute-start | bytes 1474568 | tf_op jit(solution)/shard_map/ppermute | solution.py:27
  12.8 1.7 %collective-permute-start.4 = (bf16[384,640]{1,0:T(8,128)(2,1)S(1)}, bf16[384,640]{1,0:T(8,128)(2,1)S(1)}, u32[]{:S(2)}, u32[]{:S(2)}) collective-permute-start(bf16[384,640]{1,0:T(8,128)(2,1)S(1)} %get-tuple-element.18), channel_id=1, source_target_pairs={{0,4},{1,5},{2,6},{3,7},{4,0},{5,1},{6,2},{7,3},{8,12},{9,13},{10,... | collective-permute-start | bytes 1474568 | tf_op jit(solution)/shard_map/ppermute | solution.py:27
  14.5 1.0 collective-permute-start.6
  15.5 0.0 collective-permute-start.1
  15.5 0.8 collective-permute-start
  16.3 10.7 %collective-permute-done.2.refs_2_ = bf16[384,640]{1,0:T(8,128)(2,1)S(1)} collective-permute-done((bf16[384,640]{1,0:T(8,128)(2,1)S(1)}, bf16[384,640]{1,0:T(8,128)(2,1)S(1)}, u32[]{:S(2)}, u32[]{:S(2)}) %collective-permute-start.2) | collective-permute-done | bytes 491552 | tf_op jit(solution)/shard_map/ppermute | solution.py:27
  27.1 10.1 %collective-permute-done.4.refs_4_ = bf16[384,640]{1,0:T(8,128)(2,1)S(1)} collective-permute-done((bf16[384,640]{1,0:T(8,128)(2,1)S(1)}, bf16[384,640]{1,0:T(8,128)(2,1)S(1)}, u32[]{:S(2)}, u32[]{:S(2)}) %collective-permute-start.4) | collective-permute-done | bytes 491552 | tf_op jit(solution)/shard_map/ppermute | solution.py:27
  37.2 0.5 collective-permute-start.7
  37.7 6.9 %collective-permute-done.refs_9_.c_far = bf16[384,640]{1,0:T(8,128)(2,1)S(1)} collective-permute-done((bf16[384,640]{1,0:T(8,128)(2,1)S(1)}, bf16[384,640]{1,0:T(8,128)(2,1)S(1)}, u32[]{:S(2)}, u32[]{:S(2)}) %collective-permute-start) | collective-permute-done | bytes 491552 | tf_op jit(solution)/shard_map/ppermute | solution.py:27
  44.6 4.5 %shard_map.59 = bf16[4,640,640]{2,1,0:T(8,128)(2,1)S(1)} custom-call(s32[2]{0:T(128)S(1)} %pad_add_fusion.at, bf16[384,640]{1,0:T(8,128)(2,1)S(1)} %get-tuple-element.17.refs_0_, bf16[384,640]{1,0:T(8,128)(2,1)S(1)} %collective-permute-done.1.refs_1_, bf16[384,640]{1,0:T(8,128)(2,1)S(1)} %collective-permute-done.2.refs_2_, ...), custom_call_target="tpu_custom_call" | custom-call | flops 2516582400 | bytes 8388608 | tf_op jit(solution)/shard_map/pallas_call | solution.py:143
  49.1 1.7 %copy-done.1 = bf16[4,640,640]{2,1,0:T(8,128)(2,1)} copy-done((bf16[4,640,640]{2,1,0:T(8,128)(2,1)}, bf16[4,640,640]{2,1,0:T(8,128)(2,1)S(1)}, u32[]{:S(2)}) %copy-start.1) | copy-done | bytes 3276824
  50.8 0.8 copy-done.6
  51.6 0.8 copy-done.8
  52.3 0.8 copy-done.10
  53.1 0.8 copy-done.12
  53.9 0.8 copy-done.14
  54.7 4.2 %all-gather.2.cloned.1.call-done = bf16[2560,640]{1,0:T(8,128)(2,1)} async-done(((bf16[320,640]{1,0:T(8,128)(2,1)}), bf16[2560,640]{1,0:T(8,128)(2,1)}) %all-gather.2.cloned.1.call-update) | async-done | bytes 3276816 | tf_op jit(solution)/shard_map/all_gather | solution.py:133
  59.0 0.0 reduce-scatter.2.cloned.1.call-update
  59.0 1.9 %copy-done.4 = bf16[2560,640]{1,0:T(8,128)(2,1)S(1)} copy-done((bf16[2560,640]{1,0:T(8,128)(2,1)S(1)}, bf16[2560,640]{1,0:T(8,128)(2,1)}, u32[]{:S(2)}) %copy-start.4) | copy-done | bytes 3276824
  60.9 1.0 copy-done.13
  62.0 4.3 %shard_map.60 = (bf16[2,2,384,640]{3,2,1,0:T(8,128)(2,1)S(1)}, bf16[2,2,384,640]{3,2,1,0:T(8,128)(2,1)S(1)}) custom-call(s32[2]{0:T(128)S(1)} %pad_add_fusion.at, bf16[384,640]{1,0:T(8,128)(2,1)S(1)} %copy-done.5, bf16[384,640]{1,0:T(8,128)(2,1)S(1)} %copy-done.13, bf16[4,640,640]{2,1,0:T(8,128)(2,1)S(1)} %bitcast.20), custom_call_target="tpu_custom_call" | custom-call | flops 2516582400 | bytes 8388608 | tf_op jit(solution)/shard_map/pallas_call | solution.py:148
  66.3 0.3 collective-permute-start.8
  66.6 4.2 %shard_map.62 = (bf16[384,640]{1,0:T(8,128)(2,1)}, bf16[384,640]{1,0:T(8,128)(2,1)S(1)}) custom-call(s32[2]{0:T(128)S(1)} %pad_add_fusion.at, bf16[384,640]{1,0:T(8,128)(2,1)S(1)} %get-tuple-element.17.refs_0_, bf16[384,640]{1,0:T(8,128)(2,1)S(1)} %copy-done.7, bf16[384,640]{1,0:T(8,128)(2,1)S(1)} %collective-permute-done.2.refs_2_, ...), custom_call_target="tpu_custom_call" | custom-call | flops 2516582400 | bytes 8388608 | tf_op jit(solution)/shard_map/pallas_call | solution.py:153
  70.8 0.9 collective-permute-start.12
  71.8 0.5 add_convert_fusion.keep
  72.3 1.2 slice_bitcast_fusion
  73.4 1.2 collective-permute-start.10
  74.6 0.5 collective-permute-start.11
  75.2 2.4 %collective-permute-start.9 = (bf16[384,640]{1,0:T(8,128)(2,1)}, bf16[384,640]{1,0:T(8,128)(2,1)}, u32[]{:S(2)}, u32[]{:S(2)}) collective-permute-start(bf16[384,640]{1,0:T(8,128)(2,1)} %get-tuple-element.33), channel_id=1, source_target_pairs={{0,16},{1,17},{2,18},{3,19},{4,20},{5,21},{6,22},{7,23},{8,24},{9,... | collective-permute-start | bytes 1474568 | tf_op jit(solution)/shard_map/ppermute | solution.py:27
  77.5 7.7 %collective-permute-done.12 = bf16[384,640]{1,0:T(8,128)(2,1)} collective-permute-done((bf16[384,640]{1,0:T(8,128)(2,1)}, bf16[384,640]{1,0:T(8,128)(2,1)}, u32[]{:S(2)}, u32[]{:S(2)}) %collective-permute-start.12) | collective-permute-done | bytes 491552 | tf_op jit(solution)/shard_map/ppermute | solution.py:27
  85.2 2.1 %add_convert_fusion.1 = bf16[384,640]{1,0:T(8,128)(2,1)} fusion(bf16[384,640]{1,0:T(8,128)(2,1)} %collective-permute-done.12, bf16[384,640]{1,0:T(8,128)(2,1)} %copy-done.3), kind=kLoop, calls=%fused_computation.1 | loop fusion | flops 983040 | bytes 1474560 | tf_op jit(solution)/shard_map/convert_element_type | solution.py:154
  87.3 20.0 %reduce-scatter.2.cloned.1.call-done = bf16[1,4,80,640]{3,2,1,0:T(8,128)(2,1)} async-done(((bf16[8,4,80,640]{3,2,1,0:T(8,128)(2,1)}), bf16[1,4,80,640]{3,2,1,0:T(8,128)(2,1)}) %reduce-scatter.2.cloned.1.call-update) | async-done | bytes 409616 | tf_op jit(solution)/shard_map/reduce_scatter | solution.py:145
  107.3 1.1 dynamic-slice_bitcast_fusion
  108.4 1.6 %collective-permute-start.13 = (bf16[80,640]{1,0:T(8,128)(2,1)S(1)}, bf16[80,640]{1,0:T(8,128)(2,1)S(1)}, u32[]{:S(2)}, u32[]{:S(2)}) collective-permute-start(bf16[80,640]{1,0:T(8,128)(2,1)S(1)} %get-tuple-element.28), channel_id=1, source_target_pairs={{0,1},{1,2},{2,3},{3,0},{4,5},{5,6},{6,7},{7,4},{8,9},{9,10},{10,1... | collective-permute-start | bytes 307208 | tf_op jit(solution)/shard_map/ppermute | solution.py:27
  110.0 1.7 %collective-permute-start.14 = (bf16[80,640]{1,0:T(8,128)(2,1)S(1)}, bf16[80,640]{1,0:T(8,128)(2,1)S(1)}, u32[]{:S(2)}, u32[]{:S(2)}) collective-permute-start(bf16[80,640]{1,0:T(8,128)(2,1)S(1)} %get-tuple-element.29), channel_id=1, source_target_pairs={{0,3},{1,0},{2,1},{3,2},{4,7},{5,4},{6,5},{7,6},{8,11},{9,8},{10,9... | collective-permute-start | bytes 307208 | tf_op jit(solution)/shard_map/ppermute | solution.py:27
  111.7 1.9 %collective-permute-start.15 = (bf16[80,640]{1,0:T(8,128)(2,1)S(1)}, bf16[80,640]{1,0:T(8,128)(2,1)S(1)}, u32[]{:S(2)}, u32[]{:S(2)}) collective-permute-start(bf16[80,640]{1,0:T(8,128)(2,1)S(1)} %get-tuple-element.30), channel_id=1, source_target_pairs={{0,2},{1,3},{2,0},{3,1},{4,6},{5,7},{6,4},{7,5},{8,10},{9,11},{10,... | collective-permute-start | bytes 307208 | tf_op jit(solution)/shard_map/ppermute | solution.py:27
  113.6 2.7 %shard_map.61 = bf16[384,1280]{1,0:T(8,128)(2,1)} custom-call(s32[2]{0:T(128)S(1)} %pad_add_fusion.at, bf16[2,2,384,640]{3,2,1,0:T(8,128)(2,1)S(1)} %add_convert_fusion.keep, bf16[384,640]{1,0:T(8,128)(2,1)} %collective-permute-done.9.hi, bf16[384,640]{1,0:T(8,128)(2,1)S(1)} %collective-permute-done.10.lo, bf16[384,640]{1,0:T(8,128)(2,1)} %collective-permute-done.11.both), custom_call_target="tpu_custom_call" | custom-call | bytes 8388608 | tf_op jit(solution)/shard_map/pallas_call | solution.py:151
  116.3 1.6 %collective-permute-done.15 = bf16[80,640]{1,0:T(8,128)(2,1)S(1)} collective-permute-done((bf16[80,640]{1,0:T(8,128)(2,1)S(1)}, bf16[80,640]{1,0:T(8,128)(2,1)S(1)}, u32[]{:S(2)}, u32[]{:S(2)}) %collective-permute-start.15) | collective-permute-done | bytes 102432 | tf_op jit(solution)/shard_map/ppermute | solution.py:27
  117.9 0.7 convert_add_fusion
  (34 shorter events, 0.1 us)
Async XLA Ops:
  7.2 1.2 copy-start
  7.2 8.3 %copy-start.5 = (bf16[384,640]{1,0:T(8,128)(2,1)S(1)}, bf16[384,640]{1,0:T(8,128)(2,1)}, u32[]{:S(2)}) copy-start(bf16[384,640]{1,0:T(8,128)(2,1)} %c_own.1) | copy-start | bytes 1474564
  7.2 51.8 %all-gather.2.cloned.1.call-start = ((), (), s32[]{:S(2)}) async-start(), calls=%async_computation.1 | async-start | bytes 3686400 | tf_op jit(solution)/shard_map/all_gather | solution.py:133
  9.2 98.1 %reduce-scatter.2.cloned.1.call-start = ((), (), s32[]{:S(2)}) async-start(), calls=%async_computation.2 | async-start | bytes 3686400 | tf_op jit(solution)/shard_map/reduce_scatter | solution.py:145
  9.3 1.2 copy-start.2
  11.3 15.7 %collective-permute-start.2 = (bf16[384,640]{1,0:T(8,128)(2,1)S(1)}, bf16[384,640]{1,0:T(8,128)(2,1)S(1)}, u32[]{:S(2)}, u32[]{:S(2)}) collective-permute-start(bf16[384,640]{1,0:T(8,128)(2,1)S(1)} %get-tuple-element.17.refs_0_), channel_id=1, source_target_pairs={{0,16},{1,17},{2,18},{3,19},{4,20},{5,21},{6,22},{7,23},{8,24},{9,... | collective-permute-start | bytes 1474568 | tf_op jit(solution)/shard_map/ppermute | solution.py:27
  12.8 24.4 %collective-permute-start.4 = (bf16[384,640]{1,0:T(8,128)(2,1)S(1)}, bf16[384,640]{1,0:T(8,128)(2,1)S(1)}, u32[]{:S(2)}, u32[]{:S(2)}) collective-permute-start(bf16[384,640]{1,0:T(8,128)(2,1)S(1)} %get-tuple-element.18), channel_id=1, source_target_pairs={{0,4},{1,5},{2,6},{3,7},{4,0},{5,1},{6,2},{7,3},{8,12},{9,13},{10,... | collective-permute-start | bytes 1474568 | tf_op jit(solution)/shard_map/ppermute | solution.py:27
  14.5 22.7 %collective-permute-start.6 = (bf16[384,640]{1,0:T(8,128)(2,1)S(1)}, bf16[384,640]{1,0:T(8,128)(2,1)S(1)}, u32[]{:S(2)}, u32[]{:S(2)}) collective-permute-start(bf16[384,640]{1,0:T(8,128)(2,1)S(1)} %get-tuple-element.18), channel_id=1, source_target_pairs={{0,20},{1,21},{2,22},{3,23},{4,16},{5,17},{6,18},{7,19},{8,28},{9,... | collective-permute-start | bytes 1474568 | tf_op jit(solution)/shard_map/ppermute | solution.py:27
  15.5 22.2 %collective-permute-start.1 = (bf16[384,640]{1,0:T(8,128)(2,1)S(1)}, bf16[384,640]{1,0:T(8,128)(2,1)S(1)}, u32[]{:S(2)}, u32[]{:S(2)}) collective-permute-start(bf16[384,640]{1,0:T(8,128)(2,1)S(1)} %get-tuple-element.17.refs_0_), channel_id=1, source_target_pairs={{0,8},{1,9},{2,10},{3,11},{4,12},{5,13},{6,14},{7,15},{8,0},{9,1},... | collective-permute-start | bytes 1474568 | tf_op jit(solution)/shard_map/ppermute | solution.py:27
  15.5 29.1 %collective-permute-start = (bf16[384,640]{1,0:T(8,128)(2,1)S(1)}, bf16[384,640]{1,0:T(8,128)(2,1)S(1)}, u32[]{:S(2)}, u32[]{:S(2)}) collective-permute-start(bf16[384,640]{1,0:T(8,128)(2,1)S(1)} %copy-done.5), channel_id=1, source_target_pairs={{0,4},{1,5},{2,6},{3,7},{4,0},{5,1},{6,2},{7,3},{8,12},{9,13},{10,... | collective-permute-start | bytes 1474568 | tf_op jit(solution)/shard_map/ppermute | solution.py:27
  27.1 17.5 %collective-permute-start.3 = (bf16[384,640]{1,0:T(8,128)(2,1)S(1)}, bf16[384,640]{1,0:T(8,128)(2,1)S(1)}, u32[]{:S(2)}, u32[]{:S(2)}) collective-permute-start(bf16[384,640]{1,0:T(8,128)(2,1)S(1)} %collective-permute-done.2.refs_2_), channel_id=1, source_target_pairs={{0,8},{1,9},{2,10},{3,11},{4,12},{5,13},{6,14},{7,15},{8,0},{9,1},... | collective-permute-start | bytes 1474568 | tf_op jit(solution)/shard_map/ppermute | solution.py:27
  37.2 7.4 %collective-permute-start.5 = (bf16[384,640]{1,0:T(8,128)(2,1)S(1)}, bf16[384,640]{1,0:T(8,128)(2,1)S(1)}, u32[]{:S(2)}, u32[]{:S(2)}) collective-permute-start(bf16[384,640]{1,0:T(8,128)(2,1)S(1)} %collective-permute-done.4.refs_4_), channel_id=1, source_target_pairs={{0,8},{1,9},{2,10},{3,11},{4,12},{5,13},{6,14},{7,15},{8,0},{9,1},... | collective-permute-start | bytes 1474568 | tf_op jit(solution)/shard_map/ppermute | solution.py:27
  37.2 7.4 %collective-permute-start.7 = (bf16[384,640]{1,0:T(8,128)(2,1)S(1)}, bf16[384,640]{1,0:T(8,128)(2,1)S(1)}, u32[]{:S(2)}, u32[]{:S(2)}) collective-permute-start(bf16[384,640]{1,0:T(8,128)(2,1)S(1)} %collective-permute-done.6.refs_6_), channel_id=1, source_target_pairs={{0,8},{1,9},{2,10},{3,11},{4,12},{5,13},{6,14},{7,15},{8,0},{9,1},... | collective-permute-start | bytes 1474568 | tf_op jit(solution)/shard_map/ppermute | solution.py:27
  49.1 1.7 %copy-start.1 = (bf16[4,640,640]{2,1,0:T(8,128)(2,1)}, bf16[4,640,640]{2,1,0:T(8,128)(2,1)S(1)}, u32[]{:S(2)}) copy-start(bf16[4,640,640]{2,1,0:T(8,128)(2,1)S(1)} %shard_map.59) | copy-start | bytes 9830404
  50.8 0.8 copy-start.6
  51.6 0.8 copy-start.8
  52.3 0.8 copy-start.10
  53.1 0.8 copy-start.12
  53.9 0.8 copy-start.14
  59.0 1.9 %copy-start.4 = (bf16[2560,640]{1,0:T(8,128)(2,1)S(1)}, bf16[2560,640]{1,0:T(8,128)(2,1)}, u32[]{:S(2)}) copy-start(bf16[2560,640]{1,0:T(8,128)(2,1)} %all-gather.2.cloned.1.call-done) | copy-start | bytes 9830404
  60.9 1.0 copy-start.13
  61.9 4.6 %copy-start.7 = (bf16[384,640]{1,0:T(8,128)(2,1)S(1)}, bf16[384,640]{1,0:T(8,128)(2,1)}, u32[]{:S(2)}) copy-start(bf16[384,640]{1,0:T(8,128)(2,1)} %copy-done.6) | copy-start | bytes 1474564
  62.0 4.6 %copy-start.9 = (bf16[384,640]{1,0:T(8,128)(2,1)S(1)}, bf16[384,640]{1,0:T(8,128)(2,1)}, u32[]{:S(2)}) copy-start(bf16[384,640]{1,0:T(8,128)(2,1)} %copy-done.8) | copy-start | bytes 1474564
  62.0 4.6 %copy-start.11 = (bf16[384,640]{1,0:T(8,128)(2,1)S(1)}, bf16[384,640]{1,0:T(8,128)(2,1)}, u32[]{:S(2)}) copy-start(bf16[384,640]{1,0:T(8,128)(2,1)} %copy-done.10) | copy-start | bytes 1474564
  62.0 4.6 %copy-start.15 = (bf16[384,640]{1,0:T(8,128)(2,1)S(1)}, bf16[384,640]{1,0:T(8,128)(2,1)}, u32[]{:S(2)}) copy-start(bf16[384,640]{1,0:T(8,128)(2,1)} %copy-done.14) | copy-start | bytes 1474564
  66.3 5.5 %collective-permute-start.8 = (bf16[2,2,384,640]{3,2,1,0:T(8,128)(2,1)S(1)}, bf16[2,2,384,640]{3,2,1,0:T(8,128)(2,1)S(1)}, u32[]{:S(2)}, u32[]{:S(2)}) collective-permute-start(bf16[2,2,384,640]{3,2,1,0:T(8,128)(2,1)S(1)} %get-tuple-element.21), channel_id=1, source_target_pairs={{0,8},{1,9},{2,10},{3,11},{4,12},{5,13},{6,14},{7,15},{8,0},{9,1},... | collective-permute-start | bytes 5898248 | tf_op jit(solution)/shard_map/ppermute | solution.py:27
  70.8 1.5 %copy-start.3 = (bf16[384,640]{1,0:T(8,128)(2,1)}, bf16[384,640]{1,0:T(8,128)(2,1)S(1)}, u32[]{:S(2)}) copy-start(bf16[384,640]{1,0:T(8,128)(2,1)S(1)} %get-tuple-element.23) | copy-start | bytes 1474564
  70.8 14.4 %collective-permute-start.12 = (bf16[384,640]{1,0:T(8,128)(2,1)}, bf16[384,640]{1,0:T(8,128)(2,1)}, u32[]{:S(2)}, u32[]{:S(2)}) collective-permute-start(bf16[384,640]{1,0:T(8,128)(2,1)} %get-tuple-element.24), channel_id=1, source_target_pairs={{0,4},{1,5},{2,6},{3,7},{4,0},{5,1},{6,2},{7,3},{8,12},{9,13},{10,... | collective-permute-start | bytes 1474568 | tf_op jit(solution)/shard_map/ppermute | solution.py:27
  73.4 38.3 %collective-permute-start.10 = (bf16[384,640]{1,0:T(8,128)(2,1)}, bf16[384,640]{1,0:T(8,128)(2,1)S(1)}, u32[]{:S(2)}, u32[]{:S(2)}) collective-permute-start(bf16[384,640]{1,0:T(8,128)(2,1)} %get-tuple-element.32), channel_id=1, source_target_pairs={{0,4},{1,5},{2,6},{3,7},{4,0},{5,1},{6,2},{7,3},{8,12},{9,13},{10,... | collective-permute-start | bytes 1474568 | tf_op jit(solution)/shard_map/ppermute | solution.py:27
  74.6 38.9 %collective-permute-start.11 = (bf16[384,640]{1,0:T(8,128)(2,1)}, bf16[384,640]{1,0:T(8,128)(2,1)}, u32[]{:S(2)}, u32[]{:S(2)}) collective-permute-start(bf16[384,640]{1,0:T(8,128)(2,1)} %get-tuple-element.31), channel_id=1, source_target_pairs={{0,20},{1,21},{2,22},{3,23},{4,16},{5,17},{6,18},{7,19},{8,28},{9,... | collective-permute-start | bytes 1474568 | tf_op jit(solution)/shard_map/ppermute | solution.py:27
  75.2 38.4 %collective-permute-start.9 = (bf16[384,640]{1,0:T(8,128)(2,1)}, bf16[384,640]{1,0:T(8,128)(2,1)}, u32[]{:S(2)}, u32[]{:S(2)}) collective-permute-start(bf16[384,640]{1,0:T(8,128)(2,1)} %get-tuple-element.33), channel_id=1, source_target_pairs={{0,16},{1,17},{2,18},{3,19},{4,20},{5,21},{6,22},{7,23},{8,24},{9,... | collective-permute-start | bytes 1474568 | tf_op jit(solution)/shard_map/ppermute | solution.py:27
  108.4 7.9 %collective-permute-start.13 = (bf16[80,640]{1,0:T(8,128)(2,1)S(1)}, bf16[80,640]{1,0:T(8,128)(2,1)S(1)}, u32[]{:S(2)}, u32[]{:S(2)}) collective-permute-start(bf16[80,640]{1,0:T(8,128)(2,1)S(1)} %get-tuple-element.28), channel_id=1, source_target_pairs={{0,1},{1,2},{2,3},{3,0},{4,5},{5,6},{6,7},{7,4},{8,9},{9,10},{10,1... | collective-permute-start | bytes 307208 | tf_op jit(solution)/shard_map/ppermute | solution.py:27
  110.0 6.2 %collective-permute-start.14 = (bf16[80,640]{1,0:T(8,128)(2,1)S(1)}, bf16[80,640]{1,0:T(8,128)(2,1)S(1)}, u32[]{:S(2)}, u32[]{:S(2)}) collective-permute-start(bf16[80,640]{1,0:T(8,128)(2,1)S(1)} %get-tuple-element.29), channel_id=1, source_target_pairs={{0,3},{1,0},{2,1},{3,2},{4,7},{5,4},{6,5},{7,6},{8,11},{9,8},{10,9... | collective-permute-start | bytes 307208 | tf_op jit(solution)/shard_map/ppermute | solution.py:27
  111.7 6.2 %collective-permute-start.15 = (bf16[80,640]{1,0:T(8,128)(2,1)S(1)}, bf16[80,640]{1,0:T(8,128)(2,1)S(1)}, u32[]{:S(2)}, u32[]{:S(2)}) collective-permute-start(bf16[80,640]{1,0:T(8,128)(2,1)S(1)} %get-tuple-element.30), channel_id=1, source_target_pairs={{0,2},{1,3},{2,0},{3,1},{4,6},{5,7},{6,4},{7,5},{8,10},{9,11},{10,... | collective-permute-start | bytes 307208 | tf_op jit(solution)/shard_map/ppermute | solution.py:27
Sparse Core Ops, SparseCore 0:
  9.8 49.1 all-gather.1
  61.5 45.7 reduce-scatter.1
